TPU v7x, 512 devices: a whole 4x4x16 slice. The times are simulated.
512 devices in a mesh: gx: 16 (over z), gy: 16 (over x, y), gz: 2 (over core).
Axes of the slice: x: 4, y: 4, z: 16, core: 2. Of those that a mesh axis runs over, the one named last changes fastest.
Arguments:
- moment: bfloat16 [1024, 1024, 1024], P('gx', 'gy', 'gz'), may hold values from -0.625 to 0.625
- factor_start: bfloat16 [1024, 128], replicated, may hold values from -6 to 6
Outputs:
- factor_out: float32 [1024, 128], P('gx')
All inputs are finite; a program needn't handle non-finite values.
Results may differ from a plain program's by a relative error of at most 0.0005.
Values may be sent and summed in bfloat16 or wider, within the bound.
No kernel may reach another device: no remote copies, remote signals or barrier semaphores. Data moves between devices by JAX's collectives and lax.ppermute only.
A program may use at most 64 MiB of HBM per device.

v0:
```python
import jax
import jax.numpy as jnp
from jax import lax
from jax.sharding import PartitionSpec as P


def local(moment, factor_start):
    rows_i, rows_j, rows_k = moment.shape
    order, rank = factor_start.shape
    idx_x = lax.axis_index("gx")
    idx_z = lax.axis_index("gz")
    scale_n = 1.0 / order**0.5
    krows = lax.dynamic_slice_in_dim(factor_start, idx_z * rows_k, rows_k, 0)
    partial_y = jnp.einsum("ijk,kb->ijb", moment, krows, preferred_element_type=jnp.float32)
    ysum = lax.psum_scatter(partial_y.astype(jnp.bfloat16), "gz", scatter_dimension=2, tiled=True)
    row_start = idx_x * rows_i
    out = jnp.einsum(
        "ijb,ja->iba",
        lax.all_to_all(ysum, "gy", split_axis=2, concat_axis=1, tiled=True),
        factor_start,
        preferred_element_type=jnp.float32,
    )
    ztens = (out * scale_n).astype(jnp.bfloat16)
    here_rows = ztens.shape[0]
    irows = lax.dynamic_slice_in_dim(factor_start, row_start, here_rows, 0)
    cpart = jnp.einsum("iba,ir->bar", ztens, irows, preferred_element_type=jnp.float32)
    csum = lax.psum(cpart, "gx")
    cgram = (csum * scale_n).astype(jnp.bfloat16)
    vpart = jnp.einsum("iba,bar->ir", ztens, cgram, preferred_element_type=jnp.float32)
    vnew = lax.psum(vpart, ("gy", "gz")) / rank
    total = lax.psum(jnp.sum(vnew * vnew), "gx")
    scaled = vnew * lax.rsqrt(total / (order * rank) + 1e-06)
    return scaled


def solution(mesh):
    in_specs = (P("gx", "gy", "gz"), P())
    out_specs = P("gx", None)
    return jax.shard_map(local, mesh=mesh, in_specs=in_specs, out_specs=out_specs, check_vma=False)
```

profile of v0, /device:TPU:32, one launch (start us, length us, event | category | flops | bytes accessed | tf_op | source)
XLA Modules:
  0.0 360.8 jit_solution(397070755710269224)
XLA Ops:
  6.5 0.0 copy-start
  6.5 0.0 reduce-scatter.4.cloned.1.call-start
  6.5 0.9 copy-done
  7.5 3.4 fusion
  10.9 3.0 copy.8
  13.9 2.5 reshape.4
  16.4 0.0 reduce-scatter.4.cloned.1.call-update
  16.4 23.2 %reduce-scatter.4.cloned.1.call-done = bf16[64,4096]{1,0:T(8,128)(2,1)} async-done(((bf16[128,4096]{1,0:T(8,128)(2,1)}), bf16[64,4096]{1,0:T(8,128)(2,1)}) %reduce-scatter.4.cloned.1.call-update) | async-done | bytes 524304
  39.7 2.1 reshape.5
  41.7 0.1 bitcast_bitcast_fusion
  41.8 1.5 reshape.6
  43.3 6.8 %all-to-all-start = ((bf16[16,2,8192]{2,1,0:T(2,128)(2,1)}), bf16[16,2,8192]{2,1,0:T(2,128)(2,1)S(1)}, u32[]{:S(2)}, u32[]{:S(2)}) async-start(bf16[16,2,8192]{2,1,0:T(2,128)(2,1)} %reshape.6), calls=%async_computation | async-start | bytes 1048576 | tf_op jit(solution)/shard_map/all_to_all | solution.py:19
  50.1 0.0 all-reduce.2.cloned.1.call-start
  50.2 11.9 %all-to-all-done = bf16[16,2,8192]{2,1,0:T(2,128)(2,1)S(1)} async-done(((bf16[16,2,8192]{2,1,0:T(2,128)(2,1)}), bf16[16,2,8192]{2,1,0:T(2,128)(2,1)S(1)}, u32[]{:S(2)}, u32[]{:S(2)}) %all-to-all-start) | async-done | bytes 524320 | tf_op jit(solution)/shard_map/all_to_all | solution.py:19
  62.1 0.7 reshape.7
  62.8 0.7 copy.7
  63.5 0.7 all_to_all.16
  64.2 0.3 fusion.1
  64.5 0.9 fusion.6
  65.4 0.0 all-reduce.2.cloned.1.call-update
  65.4 133.3 %all-reduce.2.cloned.1.call-done = f32[4,128,128]{2,1,0:T(8,128)} async-done(((f32[4,128,128]{2,1,0:T(8,128)}), f32[4,128,128]{2,1,0:T(8,128)}) %all-reduce.2.cloned.1.call-update) | async-done | bytes 262160 | tf_op jit(solution)/shard_map/psum | solution.py:27
  198.7 1.1 convolution_bitcast_fusion
  199.8 123.8 %psum.22 = f32[64,128]{1,0:T(8,128)S(1)} all-reduce(f32[64,128]{1,0:T(8,128)S(1)} %convolution_bitcast_fusion), channel_id=1, replica_groups=mesh['gx'=16,'gy'=16,'gz'=2] {'gy','gz'}, use_global_device_ids=true, to_apply=%region_2.0 | all-reduce | flops 8192 | bytes 65536 | tf_op jit(solution)/shard_map/psum | solution.py:30
  323.6 0.6 multiply_reduce_fusion
  324.2 28.4 %psum.23 = f32[]{:T(128)} all-reduce(f32[]{:T(128)} %multiply_reduce_fusion), channel_id=1, replica_groups=mesh['gx'=16,'gy'=16,'gz'=2] {'gx'}, use_global_device_ids=true, to_apply=%region_4.0 | all-reduce | flops 1 | bytes 8 | tf_op jit(solution)/shard_map/psum | solution.py:31
  353.3 0.6 broadcast_multiply_fusion
Async XLA Ops:
  6.5 1.0 copy-start
  6.5 33.2 %reduce-scatter.4.cloned.1.call-start = ((), (), s32[]{:S(2)}) async-start(), calls=%async_computation.3 | async-start | bytes 1572864
  43.3 18.8 %all-to-all-start = ((bf16[16,2,8192]{2,1,0:T(2,128)(2,1)}), bf16[16,2,8192]{2,1,0:T(2,128)(2,1)S(1)}, u32[]{:S(2)}, u32[]{:S(2)}) async-start(bf16[16,2,8192]{2,1,0:T(2,128)(2,1)} %reshape.6), calls=%async_computation | async-start | bytes 1048576 | tf_op jit(solution)/shard_map/all_to_all | solution.py:19
  50.1 148.6 %all-reduce.2.cloned.1.call-start = ((), (), s32[]{:S(2)}) async-start(), calls=%async_computation.2 | async-start | bytes 524288 | tf_op jit(solution)/shard_map/psum | solution.py:27
Sparse Core Ops, SparseCore 0:
  16.6 23.0 reduce-scatter.3
  65.5 133.1 all-reduce.1
where the time goes:
time: 361 us
  waiting for transfers between devices  169 us (47%)
  blocking collectives  152 us (42%)
  between operations  14.2 us (4%)
  local copies, waits for them, and re-layouts  12.1 us (3%)
  starting transfers between devices  6.85 us (2%)
  matrix products  5.75 us (2%)
    psum x1, waiting for transfers between devices, local(): csum = lax.psum(cpart, 'gx')  133 us
    psum x1, blocking collectives, local(): vnew = lax.psum(vpart, ('gy', 'gz')) / rank  124 us
    psum x1, blocking collectives, local(): total = lax.psum(jnp.sum(vnew * vnew), 'gx')  28.4 us
    unnamed x3, waiting for transfers between devices  23.3 us
    all_to_all x1, waiting for transfers between devices, local(): lax.all_to_all(ysum, 'gy', split_axis=2, concat_axis=1, tiled=True)  11.9 us
    unnamed x8, local copies, waits for them, and re-layouts  10.7 us
  transfers between devices with their start and end apart: 3, of which 3 were waited for; matrix products, arithmetic and copies ran while one was open for 0% of the time, Pallas kernels for 0%

commit v1 on v0

v1 whole, which is shorter than its diff:
```python
import jax
import jax.numpy as jnp
from jax import lax
from jax.experimental import pallas as pl
from jax.experimental.pallas import tpu as pltpu
from jax.sharding import PartitionSpec as P

F32 = jnp.float32
BF16 = jnp.bfloat16
MIB = 1 << 20
VMEM = pl.BlockSpec(memory_space=pltpu.VMEM)
SMEM = pl.BlockSpec(memory_space=pltpu.SMEM)


def params(mib):
    return pltpu.CompilerParams(vmem_limit_bytes=mib * MIB)


PAIRS = 8


def y_kernel(half_ref, lo_ref, hi_ref, u_ref, out_ref, ut_ref):
    del half_ref

    @pl.when(pl.program_id(0) == 0)
    def _():
        ut_ref[...] = u_ref[...].T

    ut = ut_ref[...]

    def one(p):
        rows = jnp.concatenate([lo_ref[p], hi_ref[p]], axis=0)
        y = lax.dot_general(ut, rows, (((1,), (1,)), ((), ())), preferred_element_type=F32)
        return y.reshape(16, 8, 128)

    for p in range(0, PAIRS, 2):
        out_ref[:, 8 * p : 8 * p + 16, :] = jnp.concatenate([one(p), one(p + 1)], axis=1).astype(BF16)


def y_half(half, core, moment, factor):
    steps = 16 // PAIRS
    return pl.pallas_call(
        y_kernel,
        out_shape=jax.ShapeDtypeStruct((16, 128, 128), BF16),
        grid_spec=pltpu.PrefetchScalarGridSpec(
            num_scalar_prefetch=1,
            grid=(steps,),
            in_specs=[
                pl.BlockSpec((PAIRS, 64, 512), lambda t, s: (s[0] * 2 * steps + t, 0, 0)),
                pl.BlockSpec((PAIRS, 64, 512), lambda t, s: (s[0] * 2 * steps + steps + t, 0, 0)),
                pl.BlockSpec((512, 128), lambda t, s: (s[1], 0)),
            ],
            out_specs=pl.BlockSpec((16, 8 * PAIRS, 128), lambda t, s: (0, t, 0)),
            scratch_shapes=[pltpu.VMEM((128, 512), BF16)],
        ),
        compiler_params=params(56),
        name="y_half",
    )(jnp.stack([half, core]).astype(jnp.int32), moment, moment, factor)


def z_kernel(y_ref, u_ref, out_ref, w_ref, z_ref):
    w_ref[...] = jnp.zeros(w_ref.shape, BF16)
    for s in range(16):
        block = u_ref[64 * s : 64 * s + 64, :]
        w_ref[128 * s : 128 * s + 64, 0:128] = block
        w_ref[128 * s + 64 : 128 * s + 128, 128:256] = block
    lhs = jnp.concatenate([y_ref[s] for s in range(16)], axis=1)
    z = jnp.dot(lhs, w_ref[...], preferred_element_type=F32) * (1.0 / 32.0)
    z_ref[0] = z[:, 0:128]
    z_ref[1] = z[:, 128:256]
    for b in range(8):
        zb = [z_ref[i2, pl.ds(b, 16, stride=8), :] for i2 in range(2)]
        parts = []
        for q in range(4):
            cut = [
                zb[i2][8 * iph : 8 * iph + 8, 32 * q : 32 * q + 32]
                for i2 in range(2)
                for iph in range(2)
            ]
            parts.append(jnp.concatenate(cut, axis=1))
        out_ref[32 * b : 32 * b + 32, :] = jnp.concatenate(parts, axis=0).astype(BF16)


def v_kernel(z_ref, u_ref, out_ref, w_ref, v_ref):
    zt = z_ref[...]
    u = u_ref[...].astype(F32).reshape(32, 4, 8, 128)
    uw = jnp.concatenate([u[:, s].reshape(256, 128) for s in range(4)], axis=1).astype(BF16)
    full = lax.dot_general(zt, uw, (((0,), (0,)), ((), ())), preferred_element_type=F32)
    c = full[0:32, 0:128]
    for s in range(1, 4):
        c = c + full[32 * s : 32 * s + 32, 128 * s : 128 * s + 128]
    c = (c * (1.0 / 32.0)).astype(BF16)
    w_ref[...] = jnp.zeros(w_ref.shape, BF16)
    for s in range(4):
        w_ref[32 * s : 32 * s + 32, 128 * s : 128 * s + 128] = c
    v = jnp.dot(zt, w_ref[...], preferred_element_type=F32)
    for s in range(4):
        v_ref[s] = v[:, 128 * s : 128 * s + 128]
        for row in range(8):
            out_ref[8 * s + row] = v_ref[s, pl.ds(row, 32, stride=8), :]


def sum_kernel(in_ref, out_ref):
    total = jnp.sum(in_ref[...], axis=0)
    out_ref[...] = jnp.broadcast_to(total[None], out_ref.shape)


def rows_kernel(idx_ref, in_ref, out_ref, v_ref):
    v = jnp.sum(in_ref[...], axis=0)
    v_ref[...] = v
    squares = jnp.sum(v * v, axis=0, keepdims=True)
    own = v_ref[pl.ds(2 * idx_ref[0], 2), :]
    block = jnp.concatenate([own, squares, jnp.zeros((5, 128), F32)], axis=0)
    out_ref[...] = jnp.broadcast_to(block[None], out_ref.shape)


def final_kernel(in_ref, out_ref):
    total = jnp.sum(in_ref[pl.ds(2, 32, stride=8), :]) * (1.0 / (128.0 * 128.0))
    scale = lax.rsqrt(total / (1024 * 128) + 1e-06) * (1.0 / 128.0)
    out_ref[0:32, :] = in_ref[pl.ds(0, 32, stride=8), :] * scale
    out_ref[32:64, :] = in_ref[pl.ds(1, 32, stride=8), :] * scale


def call(kernel, out, specs, scratch, mib, name):
    return pl.pallas_call(
        kernel,
        out_shape=jax.ShapeDtypeStruct(*out),
        in_specs=specs,
        out_specs=VMEM,
        scratch_shapes=scratch,
        compiler_params=params(mib),
        name=name,
    )


def local(moment, factor):
    plane = ("gy", "gz")
    idx_x = lax.axis_index("gx").astype(jnp.int32).reshape(1)
    core = lax.axis_index("gz")
    there = y_half(1 - core, core, moment, factor)
    came = lax.ppermute(there, "gz", [(0, 1), (1, 0)])
    here = y_half(core, core, moment, factor)
    y = (here.astype(F32) + came.astype(F32)).astype(BF16)
    y = lax.all_to_all(y, "gy", 0, 0, tiled=True)
    z = call(
        z_kernel,
        ((256, 128), BF16),
        [VMEM, VMEM],
        [pltpu.VMEM((2048, 256), BF16), pltpu.VMEM((2, 128, 128), F32)],
        8,
        "z_block",
    )(y, factor)
    z = lax.all_to_all(z.reshape(32, 8, 128), ("gx", "gz"), 0, 0, tiled=True)
    v = call(
        v_kernel,
        ((32, 32, 128), F32),
        [VMEM, VMEM],
        [pltpu.VMEM((128, 512), BF16), pltpu.VMEM((4, 256, 128), F32)],
        8,
        "v_part",
    )(z.reshape(256, 128), factor)
    v = lax.all_to_all(v, plane, 0, 0, tiled=True)
    v = call(sum_kernel, ((16, 32, 128), F32), [VMEM], [], 8, "v_sum_plane")(v)
    v = lax.all_to_all(v, "gx", 0, 0, tiled=True)
    v = call(
        rows_kernel, ((32, 8, 128), F32), [SMEM, VMEM], [pltpu.VMEM((32, 128), F32)], 8, "v_rows"
    )(idx_x, v)
    v = lax.all_to_all(v, plane, 0, 0, tiled=True)
    return call(final_kernel, ((64, 128), F32), [VMEM], [], 8, "scaled")(v.reshape(256, 128))


def solution(mesh):
    in_specs = (P("gx", "gy", "gz"), P())
    out_specs = P("gx", None)
    return jax.shard_map(local, mesh=mesh, in_specs=in_specs, out_specs=out_specs, check_vma=False)
```

time: 361 us -> 113 us (0.31)
  the two profiles are of different devices: /device:TPU:32 before, /device:TPU:1 now
where the time goes in v1:
time: 113 us
  blocking collectives  72.7 us (64%)
  waiting for transfers between devices  15.6 us (14%)
  starting transfers between devices  12.3 us (11%)
  Pallas kernels  9.96 us (9%)
  other arithmetic  2.32 us (2%)
    all_to_all x2, blocking collectives, local(): v = lax.all_to_all(v, plane, 0, 0, tiled=True)  30.9 us
    all_to_all x1, blocking collectives, local(): z = lax.all_to_all(z.reshape(32, 8, 128), ('gx', 'gz'), 0, 0, tiled=True)  28.1 us
    all_to_all x1, waiting for transfers between devices, local(): v = lax.all_to_all(v, 'gx', 0, 0, tiled=True)  15.6 us
    all_to_all x1, blocking collectives, local(): y = lax.all_to_all(y, 'gy', 0, 0, tiled=True)  13.6 us
    ppermute x1, starting transfers between devices, local(): came = lax.ppermute(there, 'gz', [(0, 1), (1, 0)])  8.78 us
    pallas_call x2, Pallas kernels, y_half(): pl.pallas_call(y_kernel, out_shape=jax.ShapeDtypeStruct((16, 128, 128), B...  7.38 us
    all_to_all x1, starting transfers between devices, local(): v = lax.all_to_all(v, 'gx', 0, 0, tiled=True)  3.53 us
  transfers between devices with their start and end apart: 2, of which 1 were waited for; matrix products, arithmetic and copies ran while one was open for 0% of the time, Pallas kernels for 3%

profile of v1, /device:TPU:1, one launch (start us, length us, event | category | flops | bytes accessed | tf_op | source)
XLA Modules:
  0.0 112.9 jit_solution(17276218438105969669)
XLA Ops:
  0.0 0.6 pad_add_fusion.1.half_ref
  0.6 3.6 %y_half.3 = bf16[16,128,128]{2,1,0:T(8,128)(2,1)} custom-call(s32[2]{0:T(128)} %pad_add_fusion.1.half_ref, bf16[64,64,512]{2,1,0:T(8,128)(2,1)} %hi_ref.3, bf16[64,64,512]{2,1,0:T(8,128)(2,1)} %hi_ref.3, bf16[1024,128]{1,0:T(8,128)(2,1)} %u_ref.7), custom_call_target="tpu_custom_call" | custom-call | tf_op jit(solution)/shard_map/y_half/pallas_call | solution.py:42
  4.2 8.8 %collective-permute-start = (bf16[16,128,128]{2,1,0:T(8,128)(2,1)}, bf16[16,128,128]{2,1,0:T(8,128)(2,1)S(1)}, u32[]{:S(2)}, u32[]{:S(2)}) collective-permute-start(bf16[16,128,128]{2,1,0:T(8,128)(2,1)} %y_half.3), channel_id=1, source_target_pairs={{0,1},{1,0},{2,3},{3,2},{4,5},{5,4},{6,7},{7,6},{8,9},{9,8},{10,11... | collective-permute-start | bytes 1572872 | tf_op jit(solution)/shard_map/ppermute | solution.py:141
  13.0 0.6 pad_add_fusion.half_ref
  13.6 0.0 copy-start
  13.6 3.7 %y_half.2 = bf16[16,128,128]{2,1,0:T(8,128)(2,1)} custom-call(s32[2]{0:T(128)} %pad_add_fusion.half_ref, bf16[64,64,512]{2,1,0:T(8,128)(2,1)} %hi_ref.3, bf16[64,64,512]{2,1,0:T(8,128)(2,1)} %hi_ref.3, bf16[1024,128]{1,0:T(8,128)(2,1)} %u_ref.7), custom_call_target="tpu_custom_call" | custom-call | tf_op jit(solution)/shard_map/y_half/pallas_call | solution.py:42
  17.3 0.0 collective-permute-done
  17.3 1.2 %add_convert_fusion = bf16[16,128,128]{2,1,0:T(8,128)(2,1)S(1)} fusion(bf16[16,128,128]{2,1,0:T(8,128)(2,1)S(1)} %collective-permute-done, bf16[16,128,128]{2,1,0:T(8,128)(2,1)} %y_half.2), kind=kLoop, calls=%fused_computation | loop fusion | flops 1048576 | bytes 1572864 | tf_op jit(solution)/shard_map/convert_element_type | solution.py:143
  18.5 13.6 %all_to_all.25.y_ref = bf16[16,128,128]{2,1,0:T(8,128)(2,1)S(1)} all-to-all(bf16[16,128,128]{2,1,0:T(8,128)(2,1)S(1)} %add_convert_fusion), channel_id=1, replica_groups=mesh['gx'=16,'gy'=16,'gz'=2] {'gy'}, dimensions={0} | all-to-all | bytes 1048576 | tf_op jit(solution)/shard_map/all_to_all | solution.py:144
  32.1 0.0 copy-done
  32.1 0.5 z_block.1
  32.7 28.1 %all_to_all.26 = bf16[32,8,128]{2,1,0:T(8,128)(2,1)S(1)} all-to-all(bf16[32,8,128]{2,1,0:T(8,128)(2,1)S(1)} %bitcast.7), channel_id=1, replica_groups=mesh['gx'=16,'gy'=16,'gz'=2] {'gx','gz'}, dimensions={0} | all-to-all | bytes 131072 | tf_op jit(solution)/shard_map/all_to_all | solution.py:153
  60.8 0.5 v_part.1
  61.3 16.5 %all_to_all.27.in_ref = f32[32,32,128]{2,1,0:T(8,128)S(1)} all-to-all(f32[32,32,128]{2,1,0:T(8,128)S(1)} %v_part.1), channel_id=1, replica_groups=mesh['gx'=16,'gy'=16,'gz'=2] {'gy','gz'}, dimensions={0} | all-to-all | bytes 1048576 | tf_op jit(solution)/shard_map/all_to_all | solution.py:162
  77.8 0.8 v_sum_plane.1
  78.5 3.5 %all-to-all-start.3 = ((f32[16,32,128]{2,1,0:T(8,128)}), f32[16,32,128]{2,1,0:T(8,128)S(1)}, u32[]{:S(2)}, u32[]{:S(2)}) async-start(f32[16,32,128]{2,1,0:T(8,128)} %v_sum_plane.1), calls=%async_computation.3 | async-start | bytes 524288 | tf_op jit(solution)/shard_map/all_to_all | solution.py:164
  82.1 15.6 %all-to-all-done.3.in_ref = f32[16,32,128]{2,1,0:T(8,128)S(1)} async-done(((f32[16,32,128]{2,1,0:T(8,128)}), f32[16,32,128]{2,1,0:T(8,128)S(1)}, u32[]{:S(2)}, u32[]{:S(2)}) %all-to-all-start.3) | async-done | bytes 262176 | tf_op jit(solution)/shard_map/all_to_all | solution.py:164
  97.7 14.4 %all_to_all.28 = f32[32,8,128]{2,1,0:T(8,128)S(1)} all-to-all(f32[32,8,128]{2,1,0:T(8,128)S(1)} %v_rows.1), channel_id=1, replica_groups=mesh['gx'=16,'gy'=16,'gz'=2] {'gy','gz'}, dimensions={0} | all-to-all | bytes 262144 | tf_op jit(solution)/shard_map/all_to_all | solution.py:168
  112.1 0.8 scaled.1
  (1 shorter events, 0.0 us)
Async XLA Ops:
  4.2 13.1 %collective-permute-start = (bf16[16,128,128]{2,1,0:T(8,128)(2,1)}, bf16[16,128,128]{2,1,0:T(8,128)(2,1)S(1)}, u32[]{:S(2)}, u32[]{:S(2)}) collective-permute-start(bf16[16,128,128]{2,1,0:T(8,128)(2,1)} %y_half.3), channel_id=1, source_target_pairs={{0,1},{1,0},{2,3},{3,2},{4,5},{5,4},{6,7},{7,6},{8,9},{9,8},{10,11... | collective-permute-start | bytes 1572872 | tf_op jit(solution)/shard_map/ppermute | solution.py:141
  13.6 18.6 %copy-start = (bf16[1024,128]{1,0:T(8,128)(2,1)S(1)}, bf16[1024,128]{1,0:T(8,128)(2,1)}, u32[]{:S(2)}) copy-start(bf16[1024,128]{1,0:T(8,128)(2,1)} %u_ref.7) | copy-start | bytes 786436
  78.5 19.1 %all-to-all-start.3 = ((f32[16,32,128]{2,1,0:T(8,128)}), f32[16,32,128]{2,1,0:T(8,128)S(1)}, u32[]{:S(2)}, u32[]{:S(2)}) async-start(f32[16,32,128]{2,1,0:T(8,128)} %v_sum_plane.1), calls=%async_computation.3 | async-start | bytes 524288 | tf_op jit(solution)/shard_map/all_to_all | solution.py:164

commit v2 on v1

--- a/solution.py
+++ b/solution.py
@@ -9,6 +9,7 @@
 BF16 = jnp.bfloat16
 MIB = 1 << 20
 VMEM = pl.BlockSpec(memory_space=pltpu.VMEM)
+ANY = pl.BlockSpec(memory_space=pl.ANY)
 SMEM = pl.BlockSpec(memory_space=pltpu.SMEM)
 
 
@@ -16,46 +17,86 @@
     return pltpu.CompilerParams(vmem_limit_bytes=mib * MIB)
 
 
-PAIRS = 8
-
-
-def y_kernel(half_ref, lo_ref, hi_ref, u_ref, out_ref, ut_ref):
-    del half_ref
-
-    @pl.when(pl.program_id(0) == 0)
-    def _():
-        ut_ref[...] = u_ref[...].T
-
-    ut = ut_ref[...]
-
-    def one(p):
-        rows = jnp.concatenate([lo_ref[p], hi_ref[p]], axis=0)
-        y = lax.dot_general(ut, rows, (((1,), (1,)), ((), ())), preferred_element_type=F32)
-        return y.reshape(16, 8, 128)
-
-    for p in range(0, PAIRS, 2):
-        out_ref[:, 8 * p : 8 * p + 16, :] = jnp.concatenate([one(p), one(p + 1)], axis=1).astype(BF16)
-
-
-def y_half(half, core, moment, factor):
-    steps = 16 // PAIRS
+def y_store(ut, rows, first, out_ref):
+    y = lax.dot_general(ut, rows, (((1,), (1,)), ((), ())), preferred_element_type=F32)
+    parts = [y[:, n : n + 128].reshape(16, 8, 128) for n in range(0, y.shape[1], 128)]
+    out_ref[:, 8 * first : 8 * (first + len(parts)), :] = jnp.concatenate(parts, axis=1).astype(BF16)
+
+
+CHUNK = 8
+CHUNKS = 16 // CHUNK
+DOT = 2
+HALF = (CHUNKS, 2, CHUNK, 64, 512)
+
+
+def y_copies(half, m_ref, buf, sem):
+    copies = []
+    for t in range(CHUNKS):
+        for h in range(2):
+            block = m_ref.at[pl.ds(32 * half + 16 * h + CHUNK * t, CHUNK)]
+            copies.append(pltpu.make_async_copy(block, buf.at[t, h], sem.at[t, h]))
+            copies[-1].start()
+    return copies
+
+
+def y_chunk(t, ut, buf, out_ref):
+    for p in range(0, CHUNK, DOT):
+        rows = jnp.concatenate([buf[t, h, p + n] for n in range(DOT) for h in range(2)], axis=0)
+        y_store(ut, rows, CHUNK * t + p, out_ref)
+
+
+def y_there_kernel(idx_ref, m_ref, u_ref, out_ref, ut_ref, mine_ref, buf, ubuf, sem, mine_sem, usem):
+    core = lax.rem(idx_ref[0], 2)
+    ucopy = pltpu.make_async_copy(u_ref.at[pl.ds(512 * core, 512)], ubuf, usem)
+    ucopy.start()
+    copies = y_copies(1 - core, m_ref, buf, sem)
+    mine = y_copies(core, m_ref, mine_ref, mine_sem)
+    ucopy.wait()
+    ut_ref[...] = ubuf[...].T
+    for t in range(CHUNKS):
+        copies[2 * t].wait()
+        copies[2 * t + 1].wait()
+        y_chunk(t, ut_ref[...], buf, out_ref)
+    for copy in mine:
+        copy.wait()
+
+
+def y_here_kernel(m_ref, ut_ref, out_ref):
+    for t in range(CHUNKS):
+        y_chunk(t, ut_ref[...], m_ref, out_ref)
+
+
+def y_there(idx, moment, factor):
     return pl.pallas_call(
-        y_kernel,
+        y_there_kernel,
+        out_shape=[
+            jax.ShapeDtypeStruct((16, 128, 128), BF16),
+            jax.ShapeDtypeStruct((128, 512), BF16),
+            jax.ShapeDtypeStruct(HALF, BF16),
+        ],
+        in_specs=[SMEM, ANY, ANY],
+        out_specs=[VMEM, VMEM, VMEM],
+        scratch_shapes=[
+            pltpu.VMEM(HALF, BF16),
+            pltpu.VMEM((512, 128), BF16),
+            pltpu.SemaphoreType.DMA((CHUNKS, 2)),
+            pltpu.SemaphoreType.DMA((CHUNKS, 2)),
+            pltpu.SemaphoreType.DMA,
+        ],
+        compiler_params=pltpu.CompilerParams(vmem_limit_bytes=48 * MIB),
+        name="y_there",
+    )(idx, moment, factor)
+
+
+def y_here(mine, ut):
+    return pl.pallas_call(
+        y_here_kernel,
         out_shape=jax.ShapeDtypeStruct((16, 128, 128), BF16),
-        grid_spec=pltpu.PrefetchScalarGridSpec(
-            num_scalar_prefetch=1,
-            grid=(steps,),
-            in_specs=[
-                pl.BlockSpec((PAIRS, 64, 512), lambda t, s: (s[0] * 2 * steps + t, 0, 0)),
-                pl.BlockSpec((PAIRS, 64, 512), lambda t, s: (s[0] * 2 * steps + steps + t, 0, 0)),
-                pl.BlockSpec((512, 128), lambda t, s: (s[1], 0)),
-            ],
-            out_specs=pl.BlockSpec((16, 8 * PAIRS, 128), lambda t, s: (0, t, 0)),
-            scratch_shapes=[pltpu.VMEM((128, 512), BF16)],
-        ),
-        compiler_params=params(56),
-        name="y_half",
-    )(jnp.stack([half, core]).astype(jnp.int32), moment, moment, factor)
+        in_specs=[VMEM, VMEM],
+        out_specs=VMEM,
+        compiler_params=pltpu.CompilerParams(vmem_limit_bytes=16 * MIB),
+        name="y_here",
+    )(mine, ut)
 
 
 def z_kernel(y_ref, u_ref, out_ref, w_ref, z_ref):
@@ -100,25 +141,35 @@
             out_ref[8 * s + row] = v_ref[s, pl.ds(row, 32, stride=8), :]
 
 
-def sum_kernel(in_ref, out_ref):
+def sum_kernel(in_ref, out_ref, mid_ref, low_ref, tail_ref):
     total = jnp.sum(in_ref[...], axis=0)
-    out_ref[...] = jnp.broadcast_to(total[None], out_ref.shape)
+    high = total.astype(BF16).astype(F32)
+    rest = total - high
+    mid = rest.astype(BF16).astype(F32)
+    mid_ref[...] = mid
+    low_ref[...] = rest - mid
+    tail_ref[...] = jnp.zeros(tail_ref.shape, F32)
+    for d in range(16):
+        tail_ref[d, 0:2, :] = mid_ref[2 * d : 2 * d + 2, :]
+        tail_ref[d, 2:4, :] = low_ref[2 * d : 2 * d + 2, :]
+    high = jnp.broadcast_to(high[None], (16, 32, 128))
+    out_ref[...] = jnp.concatenate([high, tail_ref[...]], axis=1).astype(BF16)
 
 
 def rows_kernel(idx_ref, in_ref, out_ref, v_ref):
-    v = jnp.sum(in_ref[...], axis=0)
+    v = jnp.sum(in_ref[...].astype(F32), axis=0)
     v_ref[...] = v
-    squares = jnp.sum(v * v, axis=0, keepdims=True)
-    own = v_ref[pl.ds(2 * idx_ref[0], 2), :]
-    block = jnp.concatenate([own, squares, jnp.zeros((5, 128), F32)], axis=0)
+    squares = jnp.sum(v[0:32] * v[0:32], axis=0, keepdims=True)
+    own = v_ref[pl.ds(2 * (idx_ref[0] // 2), 2), :] + (v[32:34] + v[34:36])
+    block = jnp.concatenate([own, squares, jnp.zeros((1, 128), F32)], axis=0)
     out_ref[...] = jnp.broadcast_to(block[None], out_ref.shape)
 
 
 def final_kernel(in_ref, out_ref):
-    total = jnp.sum(in_ref[pl.ds(2, 32, stride=8), :]) * (1.0 / (128.0 * 128.0))
+    total = jnp.sum(in_ref[pl.ds(2, 32, stride=4), :]) * (1.0 / (128.0 * 128.0))
     scale = lax.rsqrt(total / (1024 * 128) + 1e-06) * (1.0 / 128.0)
-    out_ref[0:32, :] = in_ref[pl.ds(0, 32, stride=8), :] * scale
-    out_ref[32:64, :] = in_ref[pl.ds(1, 32, stride=8), :] * scale
+    out_ref[0:32, :] = in_ref[pl.ds(0, 32, stride=4), :] * scale
+    out_ref[32:64, :] = in_ref[pl.ds(1, 32, stride=4), :] * scale
 
 
 def call(kernel, out, specs, scratch, mib, name):
@@ -135,11 +186,10 @@
 
 def local(moment, factor):
     plane = ("gy", "gz")
-    idx_x = lax.axis_index("gx").astype(jnp.int32).reshape(1)
-    core = lax.axis_index("gz")
-    there = y_half(1 - core, core, moment, factor)
+    idx = (2 * lax.axis_index("gx") + lax.axis_index("gz")).astype(jnp.int32).reshape(1)
+    there, ut, mine = y_there(idx, moment, factor)
     came = lax.ppermute(there, "gz", [(0, 1), (1, 0)])
-    here = y_half(core, core, moment, factor)
+    here = y_here(mine, ut)
     y = (here.astype(F32) + came.astype(F32)).astype(BF16)
     y = lax.all_to_all(y, "gy", 0, 0, tiled=True)
     z = call(
@@ -160,13 +210,20 @@
         "v_part",
     )(z.reshape(256, 128), factor)
     v = lax.all_to_all(v, plane, 0, 0, tiled=True)
-    v = call(sum_kernel, ((16, 32, 128), F32), [VMEM], [], 8, "v_sum_plane")(v)
+    v = call(
+        sum_kernel,
+        ((16, 40, 128), BF16),
+        [VMEM],
+        [pltpu.VMEM((32, 128), F32), pltpu.VMEM((32, 128), F32), pltpu.VMEM((16, 8, 128), F32)],
+        8,
+        "v_sum_plane",
+    )(v)
     v = lax.all_to_all(v, "gx", 0, 0, tiled=True)
     v = call(
-        rows_kernel, ((32, 8, 128), F32), [SMEM, VMEM], [pltpu.VMEM((32, 128), F32)], 8, "v_rows"
-    )(idx_x, v)
+        rows_kernel, ((32, 4, 128), F32), [SMEM, VMEM], [pltpu.VMEM((40, 128), F32)], 8, "v_rows"
+    )(idx, v)
     v = lax.all_to_all(v, plane, 0, 0, tiled=True)
-    return call(final_kernel, ((64, 128), F32), [VMEM], [], 8, "scaled")(v.reshape(256, 128))
+    return call(final_kernel, ((64, 128), F32), [VMEM], [], 8, "scaled")(v.reshape(128, 128))
 
 
 def solution(mesh):

time: 113 us -> 103 us (0.912)
  waiting for transfers between devices: 15.6 us -> 0.69 us
  blocking collectives: 72.7 us -> 87.1 us
  Pallas kernels: 9.96 us -> 5.4 us
  starting transfers between devices: 12.3 us -> 8.78 us
  other arithmetic: 2.32 us -> 0.14 us
    all_to_all x0 -> x1, blocking collectives: none -> 15.7 us  [local(): v = lax.all_to_all(v, 'gx', 0, 0, tiled=True)]
    all_to_all x1 -> x0, waiting for transfers between devices: 15.6 us -> none  [local(): v = lax.all_to_all(v, 'gx', 0, 0, tiled=True)]
    pallas_call x4, Pallas kernels: 8.17 us -> 3.61 us  [the longest x1 2.69 us: y_there(): pl.pallas_call(y_there_kernel, out_shape=[jax.ShapeDtypeStruct((16, 128,...]
    all_to_all x1 -> x0, starting transfers between devices: 3.53 us -> none  [local(): v = lax.all_to_all(v, 'gx', 0, 0, tiled=True)]
    all_to_all x2, blocking collectives: 30.9 us -> 29.7 us  [local(): v = lax.all_to_all(v, plane, 0, 0, tiled=True)]
    another operation x2 -> x0, other arithmetic: 1.14 us -> none  [y_half(): jnp.stack([half, core]).astype(jnp.int32)]
  transfers between devices with their start and end apart: 2 -> 1, of which waited for: 1 -> 1; matrix products, arithmetic and copies ran while one was open for 0% -> 0% of each run, Pallas kernels for 3% -> 1%
where the time goes in v2:
time: 103 us
  blocking collectives  87.1 us (85%)
  starting transfers between devices  8.78 us (9%)
  Pallas kernels  5.4 us (5%)
    all_to_all x2, blocking collectives, local(): v = lax.all_to_all(v, plane, 0, 0, tiled=True)  29.7 us
    all_to_all x1, blocking collectives, local(): z = lax.all_to_all(z.reshape(32, 8, 128), ('gx', 'gz'), 0, 0, tiled=True)  28.9 us
    all_to_all x1, blocking collectives, local(): v = lax.all_to_all(v, 'gx', 0, 0, tiled=True)  15.7 us
    all_to_all x1, blocking collectives, local(): y = lax.all_to_all(y, 'gy', 0, 0, tiled=True)  12.9 us
    ppermute x1, starting transfers between devices, local(): came = lax.ppermute(there, 'gz', [(0, 1), (1, 0)])  8.78 us
    pallas_call x1, Pallas kernels, y_there(): pl.pallas_call(y_there_kernel, out_shape=[jax.ShapeDtypeStruct((16, 128,...  2.69 us
  transfers between devices with their start and end apart: 1, of which 1 were waited for; matrix products, arithmetic and copies ran while one was open for 0% of the time, Pallas kernels for 1%

profile of v2, /device:TPU:1, one launch (start us, length us, event | category | flops | bytes accessed | tf_op | source)
XLA Modules:
  0.0 103.1 jit_solution(9163146588194994656)
XLA Ops:
  0.0 0.0 copy-start
  0.0 0.9 copy-done
  1.0 2.7 %y_there.1 = (bf16[16,128,128]{2,1,0:T(8,128)(2,1)S(1)}, bf16[128,512]{1,0:T(8,128)(2,1)S(1)}, bf16[2,2,8,64,512]{4,3,2,1,0:T(8,128)(2,1)S(1)}) custom-call(s32[1]{0:T(128)} %bitcast.idx_ref, bf16[64,64,512]{2,1,0:T(8,128)(2,1)} %m_ref.1, bf16[1024,128]{1,0:T(8,128)(2,1)S(1)} %copy-done), custom_call_target="tpu_custom_call" | custom-call | tf_op jit(solution)/shard_map/y_there/pallas_call | solution.py:70
  3.6 8.8 %collective-permute-start = (bf16[16,128,128]{2,1,0:T(8,128)(2,1)S(1)}, bf16[16,128,128]{2,1,0:T(8,128)(2,1)S(1)}, u32[]{:S(2)}, u32[]{:S(2)}) collective-permute-start(bf16[16,128,128]{2,1,0:T(8,128)(2,1)S(1)} %get-tuple-element.10), channel_id=1, source_target_pairs={{0,1},{1,0},{2,3},{3,2},{4,5},{5,4},{6,7},{7,6},{8,9},{9,8},{10,11... | collective-permute-start | bytes 1572872 | tf_op jit(solution)/shard_map/ppermute | solution.py:191
  12.4 0.8 y_here.1
  13.3 0.7 collective-permute-done
  14.0 0.1 add_convert_fusion
  14.1 12.9 %all_to_all.25.y_ref = bf16[16,128,128]{2,1,0:T(8,128)(2,1)S(1)} all-to-all(bf16[16,128,128]{2,1,0:T(8,128)(2,1)S(1)} %add_convert_fusion), channel_id=1, replica_groups=mesh['gx'=16,'gy'=16,'gz'=2] {'gy'}, dimensions={0} | all-to-all | bytes 1048576 | tf_op jit(solution)/shard_map/all_to_all | solution.py:194
  27.0 0.5 z_block.1
  27.5 28.9 %all_to_all.26 = bf16[32,8,128]{2,1,0:T(8,128)(2,1)S(1)} all-to-all(bf16[32,8,128]{2,1,0:T(8,128)(2,1)S(1)} %bitcast.5), channel_id=1, replica_groups=mesh['gx'=16,'gy'=16,'gz'=2] {'gx','gz'}, dimensions={0} | all-to-all | bytes 131072 | tf_op jit(solution)/shard_map/all_to_all | solution.py:203
  56.4 0.5 v_part.1
  56.9 16.5 %all_to_all.27.in_ref = f32[32,32,128]{2,1,0:T(8,128)S(1)} all-to-all(f32[32,32,128]{2,1,0:T(8,128)S(1)} %v_part.1), channel_id=1, replica_groups=mesh['gx'=16,'gy'=16,'gz'=2] {'gy','gz'}, dimensions={0} | all-to-all | bytes 1048576 | tf_op jit(solution)/shard_map/all_to_all | solution.py:212
  73.4 0.1 v_sum_plane.1
  73.4 15.7 %all_to_all.28.in_ref = bf16[16,40,128]{2,1,0:T(8,128)(2,1)S(1)} all-to-all(bf16[16,40,128]{2,1,0:T(8,128)(2,1)S(1)} %v_sum_plane.1), channel_id=1, replica_groups=mesh['gx'=16,'gy'=16,'gz'=2] {'gx'}, dimensions={0} | all-to-all | bytes 327680 | tf_op jit(solution)/shard_map/all_to_all | solution.py:221
  89.1 13.2 %all_to_all.29 = f32[32,4,128]{2,1,0:T(4,128)S(1)} all-to-all(f32[32,4,128]{2,1,0:T(4,128)S(1)} %v_rows.1), channel_id=1, replica_groups=mesh['gx'=16,'gy'=16,'gz'=2] {'gy','gz'}, dimensions={0} | all-to-all | bytes 131072 | tf_op jit(solution)/shard_map/all_to_all | solution.py:225
  102.3 0.8 scaled.1
  (1 shorter events, 0.0 us)
Async XLA Ops:
  0.0 0.9 copy-start
  3.6 10.3 %collective-permute-start = (bf16[16,128,128]{2,1,0:T(8,128)(2,1)S(1)}, bf16[16,128,128]{2,1,0:T(8,128)(2,1)S(1)}, u32[]{:S(2)}, u32[]{:S(2)}) collective-permute-start(bf16[16,128,128]{2,1,0:T(8,128)(2,1)S(1)} %get-tuple-element.10), channel_id=1, source_target_pairs={{0,1},{1,0},{2,3},{3,2},{4,5},{5,4},{6,7},{7,6},{8,9},{9,8},{10,11... | collective-permute-start | bytes 1572872 | tf_op jit(solution)/shard_map/ppermute | solution.py:191

commit v3 on v2

--- a/solution.py
+++ b/solution.py
@@ -45,58 +45,56 @@
         y_store(ut, rows, CHUNK * t + p, out_ref)
 
 
-def y_there_kernel(idx_ref, m_ref, u_ref, out_ref, ut_ref, mine_ref, buf, ubuf, sem, mine_sem, usem):
+def stage_kernel(idx_ref, m_ref, theirs_ref, sem):
+    for copy in y_copies(1 - lax.rem(idx_ref[0], 2), m_ref, theirs_ref, sem):
+        copy.wait()
+
+
+def y_there_kernel(idx_ref, theirs_ref, u_ref, out_ref, ut_ref):
     core = lax.rem(idx_ref[0], 2)
-    ucopy = pltpu.make_async_copy(u_ref.at[pl.ds(512 * core, 512)], ubuf, usem)
-    ucopy.start()
-    copies = y_copies(1 - core, m_ref, buf, sem)
-    mine = y_copies(core, m_ref, mine_ref, mine_sem)
-    ucopy.wait()
-    ut_ref[...] = ubuf[...].T
+    ut_ref[...] = u_ref[pl.ds(pl.multiple_of(512 * core, 512), 512), :].T
+    for t in range(CHUNKS):
+        y_chunk(t, ut_ref[...], theirs_ref, out_ref)
+
+
+def y_here_kernel(idx_ref, m_ref, ut_ref, out_ref, buf, sem):
+    copies = y_copies(lax.rem(idx_ref[0], 2), m_ref, buf, sem)
     for t in range(CHUNKS):
         copies[2 * t].wait()
         copies[2 * t + 1].wait()
         y_chunk(t, ut_ref[...], buf, out_ref)
-    for copy in mine:
-        copy.wait()
-
-
-def y_here_kernel(m_ref, ut_ref, out_ref):
-    for t in range(CHUNKS):
-        y_chunk(t, ut_ref[...], m_ref, out_ref)
 
 
 def y_there(idx, moment, factor):
+    theirs = pl.pallas_call(
+        stage_kernel,
+        out_shape=jax.ShapeDtypeStruct(HALF, BF16),
+        in_specs=[SMEM, ANY],
+        out_specs=VMEM,
+        scratch_shapes=[pltpu.SemaphoreType.DMA((CHUNKS, 2))],
+        compiler_params=params(48),
+        name="stage",
+    )(idx, moment)
     return pl.pallas_call(
         y_there_kernel,
-        out_shape=[
-            jax.ShapeDtypeStruct((16, 128, 128), BF16),
-            jax.ShapeDtypeStruct((128, 512), BF16),
-            jax.ShapeDtypeStruct(HALF, BF16),
-        ],
-        in_specs=[SMEM, ANY, ANY],
-        out_specs=[VMEM, VMEM, VMEM],
-        scratch_shapes=[
-            pltpu.VMEM(HALF, BF16),
-            pltpu.VMEM((512, 128), BF16),
-            pltpu.SemaphoreType.DMA((CHUNKS, 2)),
-            pltpu.SemaphoreType.DMA((CHUNKS, 2)),
-            pltpu.SemaphoreType.DMA,
-        ],
-        compiler_params=pltpu.CompilerParams(vmem_limit_bytes=48 * MIB),
+        out_shape=[jax.ShapeDtypeStruct((16, 128, 128), BF16), jax.ShapeDtypeStruct((128, 512), BF16)],
+        in_specs=[SMEM, VMEM, VMEM],
+        out_specs=[VMEM, VMEM],
+        compiler_params=params(48),
         name="y_there",
-    )(idx, moment, factor)
-
-
-def y_here(mine, ut):
+    )(idx, theirs, factor)
+
+
+def y_here(idx, moment, ut):
     return pl.pallas_call(
         y_here_kernel,
         out_shape=jax.ShapeDtypeStruct((16, 128, 128), BF16),
-        in_specs=[VMEM, VMEM],
+        in_specs=[SMEM, ANY, VMEM],
         out_specs=VMEM,
-        compiler_params=pltpu.CompilerParams(vmem_limit_bytes=16 * MIB),
+        scratch_shapes=[pltpu.VMEM(HALF, BF16), pltpu.SemaphoreType.DMA((CHUNKS, 2))],
+        compiler_params=params(48),
         name="y_here",
-    )(mine, ut)
+    )(idx, moment, ut)
 
 
 def z_kernel(y_ref, u_ref, out_ref, w_ref, z_ref):
@@ -119,23 +117,29 @@
                 for iph in range(2)
             ]
             parts.append(jnp.concatenate(cut, axis=1))
-        out_ref[32 * b : 32 * b + 32, :] = jnp.concatenate(parts, axis=0).astype(BF16)
-
-
-def v_kernel(z_ref, u_ref, out_ref, w_ref, v_ref):
-    zt = z_ref[...]
-    u = u_ref[...].astype(F32).reshape(32, 4, 8, 128)
-    uw = jnp.concatenate([u[:, s].reshape(256, 128) for s in range(4)], axis=1).astype(BF16)
+        for q2 in range(2):
+            block = jnp.concatenate(parts[2 * q2 : 2 * q2 + 2], axis=0).astype(BF16)
+            out_ref[2 * b + q2] = block
+
+
+def v_kernel(idx_ref, z_ref, u_ref, out_ref, w_ref, v_ref):
+    core = lax.rem(idx_ref[0], 2)
+    z = z_ref[...].astype(F32)
+    zt = jnp.concatenate([z[:, 8 * q : 8 * q + 8].reshape(256, 128) for q in range(2)], axis=1).astype(BF16)
+    u = u_ref[...].astype(F32).reshape(16, 2, 4, 8, 128)
+    uw = [jnp.concatenate([u[:, h, s].reshape(128, 128) for h in range(2)], axis=0) for s in range(4)]
+    uw = jnp.concatenate(uw, axis=1).astype(BF16)
     full = lax.dot_general(zt, uw, (((0,), (0,)), ((), ())), preferred_element_type=F32)
-    c = full[0:32, 0:128]
-    for s in range(1, 4):
-        c = c + full[32 * s : 32 * s + 32, 128 * s : 128 * s + 128]
-    c = (c * (1.0 / 32.0)).astype(BF16)
     w_ref[...] = jnp.zeros(w_ref.shape, BF16)
-    for s in range(4):
-        w_ref[32 * s : 32 * s + 32, 128 * s : 128 * s + 128] = c
+    for q in range(2):
+        c = full[128 * q : 128 * q + 32, 0:128]
+        for s in range(1, 4):
+            c = c + full[128 * q + 32 * s : 128 * q + 32 * s + 32, 128 * s : 128 * s + 128]
+        c = (c * (1.0 / 32.0)).astype(BF16)
+        for s in range(2):
+            w_ref[pl.ds(pl.multiple_of(128 * q + 64 * core + 32 * s, 32), 32), 128 * s : 128 * s + 128] = c
     v = jnp.dot(zt, w_ref[...], preferred_element_type=F32)
-    for s in range(4):
+    for s in range(2):
         v_ref[s] = v[:, 128 * s : 128 * s + 128]
         for row in range(8):
             out_ref[8 * s + row] = v_ref[s, pl.ds(row, 32, stride=8), :]
@@ -150,8 +154,9 @@
     low_ref[...] = rest - mid
     tail_ref[...] = jnp.zeros(tail_ref.shape, F32)
     for d in range(16):
-        tail_ref[d, 0:2, :] = mid_ref[2 * d : 2 * d + 2, :]
-        tail_ref[d, 2:4, :] = low_ref[2 * d : 2 * d + 2, :]
+        for h in range(2):
+            tail_ref[d, h : h + 1, :] = mid_ref[16 * h + d : 16 * h + d + 1, :]
+            tail_ref[d, 2 + h : 3 + h, :] = low_ref[16 * h + d : 16 * h + d + 1, :]
     high = jnp.broadcast_to(high[None], (16, 32, 128))
     out_ref[...] = jnp.concatenate([high, tail_ref[...]], axis=1).astype(BF16)
 
@@ -160,16 +165,22 @@
     v = jnp.sum(in_ref[...].astype(F32), axis=0)
     v_ref[...] = v
     squares = jnp.sum(v[0:32] * v[0:32], axis=0, keepdims=True)
-    own = v_ref[pl.ds(2 * (idx_ref[0] // 2), 2), :] + (v[32:34] + v[34:36])
-    block = jnp.concatenate([own, squares, jnp.zeros((1, 128), F32)], axis=0)
-    out_ref[...] = jnp.broadcast_to(block[None], out_ref.shape)
+    block = idx_ref[0] // 2
+    own = jnp.concatenate([v_ref[pl.ds(block, 1), :], v_ref[pl.ds(16 + block, 1), :]], axis=0)
+    own = own + (v[32:34] + v[34:36])
+    message = jnp.concatenate([own, squares, jnp.zeros((1, 128), F32)], axis=0)
+    out_ref[...] = jnp.broadcast_to(message[None], out_ref.shape)
 
 
 def final_kernel(in_ref, out_ref):
     total = jnp.sum(in_ref[pl.ds(2, 32, stride=4), :]) * (1.0 / (128.0 * 128.0))
     scale = lax.rsqrt(total / (1024 * 128) + 1e-06) * (1.0 / 128.0)
-    out_ref[0:32, :] = in_ref[pl.ds(0, 32, stride=4), :] * scale
-    out_ref[32:64, :] = in_ref[pl.ds(1, 32, stride=4), :] * scale
+    for half in range(2):
+        for core in range(2):
+            for s in range(2):
+                rows = in_ref[pl.ds(64 * s + 4 * core + half, 8, stride=8), :]
+                first = 32 * half + 16 * core + 8 * s
+                out_ref[first : first + 8, :] = rows * scale
 
 
 def call(kernel, out, specs, scratch, mib, name):
@@ -187,29 +198,30 @@
 def local(moment, factor):
     plane = ("gy", "gz")
     idx = (2 * lax.axis_index("gx") + lax.axis_index("gz")).astype(jnp.int32).reshape(1)
-    there, ut, mine = y_there(idx, moment, factor)
+    there, ut = y_there(idx, moment, factor)
     came = lax.ppermute(there, "gz", [(0, 1), (1, 0)])
-    here = y_here(mine, ut)
+    here = y_here(idx, moment, ut)
     y = (here.astype(F32) + came.astype(F32)).astype(BF16)
     y = lax.all_to_all(y, "gy", 0, 0, tiled=True)
     z = call(
         z_kernel,
-        ((256, 128), BF16),
+        ((16, 16, 128), BF16),
         [VMEM, VMEM],
         [pltpu.VMEM((2048, 256), BF16), pltpu.VMEM((2, 128, 128), F32)],
         8,
         "z_block",
     )(y, factor)
-    z = lax.all_to_all(z.reshape(32, 8, 128), ("gx", "gz"), 0, 0, tiled=True)
+    z = lax.all_to_all(z, "gx", 0, 0, tiled=True)
+    z = lax.all_gather(z, "gz", axis=0, tiled=True)
     v = call(
         v_kernel,
-        ((32, 32, 128), F32),
-        [VMEM, VMEM],
-        [pltpu.VMEM((128, 512), BF16), pltpu.VMEM((4, 256, 128), F32)],
+        ((16, 32, 128), F32),
+        [SMEM, VMEM, VMEM],
+        [pltpu.VMEM((256, 256), BF16), pltpu.VMEM((2, 256, 128), F32)],
         8,
         "v_part",
-    )(z.reshape(256, 128), factor)
-    v = lax.all_to_all(v, plane, 0, 0, tiled=True)
+    )(idx, z, factor)
+    v = lax.all_to_all(v, "gy", 0, 0, tiled=True)
     v = call(
         sum_kernel,
         ((16, 40, 128), BF16),

time: 103 us -> 98.9 us (0.960)
  blocking collectives: 87.1 us -> 83.7 us
    all_to_all x2 -> x1, blocking collectives: 29.7 us -> 15.4 us  [local(): v = lax.all_to_all(v, plane, 0, 0, tiled=True)]
    all_to_all x1 -> x2, blocking collectives: 28.9 us -> 35.6 us  [the longest x1 25 us: local(): z = lax.all_to_all(z, 'gx', 0, 0, tiled=True)]
    all_gather x0 -> x1, blocking collectives: none -> 5.06 us  [local(): z = lax.all_gather(z, 'gz', axis=0, tiled=True)]
    pallas_call x1, Pallas kernels: 2.69 us -> 0.82 us  [y_there(): pl.pallas_call(y_there_kernel, out_shape=[jax.ShapeDtypeStruct((16, 128,...]
    pallas_call x2 -> x3, Pallas kernels: 1.01 us -> 2.74 us  [the longest x1 1.7 us: y_there(): pl.pallas_call(stage_kernel, out_shape=jax.ShapeDtypeStruct(HALF, BF16),...]
where the time goes in v3:
time: 98.9 us; the launch traced here: 98.6 us
  blocking collectives  83.7 us (85%)
  starting transfers between devices  8.79 us (9%)
  Pallas kernels  5.58 us (6%)
    all_to_all x1, blocking collectives, local(): z = lax.all_to_all(z, 'gx', 0, 0, tiled=True)  25 us
    all_to_all x1, blocking collectives, local(): v = lax.all_to_all(v, plane, 0, 0, tiled=True)  15.4 us
    all_to_all x1, blocking collectives, local(): v = lax.all_to_all(v, 'gx', 0, 0, tiled=True)  14.7 us
    all_to_all x1, blocking collectives, local(): y = lax.all_to_all(y, 'gy', 0, 0, tiled=True)  12.9 us
    all_to_all x1, blocking collectives, local(): v = lax.all_to_all(v, 'gy', 0, 0, tiled=True)  10.6 us
    ppermute x1, starting transfers between devices, local(): came = lax.ppermute(there, 'gz', [(0, 1), (1, 0)])  8.79 us
    all_gather x1, blocking collectives, local(): z = lax.all_gather(z, 'gz', axis=0, tiled=True)  5.06 us
  transfers between devices with their start and end apart: 1, of which 1 were waited for; matrix products, arithmetic and copies ran while one was open for 0% of the time, Pallas kernels for 1%

profile of v3, /device:TPU:1, one launch (start us, length us, event | category | flops | bytes accessed | tf_op | source)
XLA Modules:
  0.0 98.6 jit_solution(10047118999147548831)
XLA Ops:
  0.0 0.0 copy-start.1
  0.0 0.0 copy-start
  0.0 1.7 %stage.1.theirs_ref = bf16[2,2,8,64,512]{4,3,2,1,0:T(8,128)(2,1)S(1)} custom-call(s32[1]{0:T(128)} %bitcast.idx_ref, bf16[64,64,512]{2,1,0:T(8,128)(2,1)} %m_ref.3), custom_call_target="tpu_custom_call" | custom-call | tf_op jit(solution)/shard_map/stage/pallas_call | solution.py:69
  1.7 0.0 copy-done.1
  1.7 0.8 y_there.1
  2.5 8.8 %collective-permute-start = (bf16[16,128,128]{2,1,0:T(8,128)(2,1)S(1)}, bf16[16,128,128]{2,1,0:T(8,128)(2,1)S(1)}, u32[]{:S(2)}, u32[]{:S(2)}) collective-permute-start(bf16[16,128,128]{2,1,0:T(8,128)(2,1)S(1)} %get-tuple-element.8), channel_id=1, source_target_pairs={{0,1},{1,0},{2,3},{3,2},{4,5},{5,4},{6,7},{7,6},{8,9},{9,8},{10,11... | collective-permute-start | bytes 1572872 | tf_op jit(solution)/shard_map/ppermute | solution.py:202
  11.3 0.0 copy-done
  11.3 1.1 %y_here.1 = bf16[16,128,128]{2,1,0:T(8,128)(2,1)S(1)} custom-call(s32[1]{0:T(128)} %bitcast.idx_ref, bf16[64,64,512]{2,1,0:T(8,128)(2,1)S(1)} %copy-done, bf16[128,512]{1,0:T(8,128)(2,1)S(1)} %get-tuple-element.7.ut_ref), custom_call_target="tpu_custom_call" | custom-call | tf_op jit(solution)/shard_map/y_here/pallas_call | solution.py:89
  12.5 0.4 collective-permute-done
  12.9 0.1 add_convert_fusion
  13.0 12.9 %all_to_all.25.y_ref = bf16[16,128,128]{2,1,0:T(8,128)(2,1)S(1)} all-to-all(bf16[16,128,128]{2,1,0:T(8,128)(2,1)S(1)} %add_convert_fusion), channel_id=1, replica_groups=mesh['gx'=16,'gy'=16,'gz'=2] {'gy'}, dimensions={0} | all-to-all | bytes 1048576 | tf_op jit(solution)/shard_map/all_to_all | solution.py:205
  25.9 0.5 z_block.1
  26.4 25.0 %all_to_all.26 = bf16[16,16,128]{2,1,0:T(8,128)(2,1)S(1)} all-to-all(bf16[16,16,128]{2,1,0:T(8,128)(2,1)S(1)} %z_block.1), channel_id=1, replica_groups=mesh['gx'=16,'gy'=16,'gz'=2] {'gx'}, dimensions={0} | all-to-all | bytes 131072 | tf_op jit(solution)/shard_map/all_to_all | solution.py:214
  51.5 5.1 %all_gather.3.z_ref = bf16[32,16,128]{2,1,0:T(8,128)(2,1)S(1)} all-gather(bf16[16,16,128]{2,1,0:T(8,128)(2,1)S(1)} %all_to_all.26), channel_id=1, replica_groups=mesh['gx'=16,'gy'=16,'gz'=2] {'gz'}, dimensions={0}, use_global_device_ids=true | all-gather | bytes 196608 | tf_op jit(solution)/shard_map/all_gather | solution.py:215
  56.5 0.5 v_part.1
  57.0 10.6 %all_to_all.27.in_ref = f32[16,32,128]{2,1,0:T(8,128)S(1)} all-to-all(f32[16,32,128]{2,1,0:T(8,128)S(1)} %v_part.1), channel_id=1, replica_groups=mesh['gx'=16,'gy'=16,'gz'=2] {'gy'}, dimensions={0} | all-to-all | bytes 524288 | tf_op jit(solution)/shard_map/all_to_all | solution.py:224
  67.6 0.1 v_sum_plane.1
  67.7 14.7 %all_to_all.28.in_ref = bf16[16,40,128]{2,1,0:T(8,128)(2,1)S(1)} all-to-all(bf16[16,40,128]{2,1,0:T(8,128)(2,1)S(1)} %v_sum_plane.1), channel_id=1, replica_groups=mesh['gx'=16,'gy'=16,'gz'=2] {'gx'}, dimensions={0} | all-to-all | bytes 327680 | tf_op jit(solution)/shard_map/all_to_all | solution.py:233
  82.4 15.4 %all_to_all.29 = f32[32,4,128]{2,1,0:T(4,128)S(1)} all-to-all(f32[32,4,128]{2,1,0:T(4,128)S(1)} %v_rows.1), channel_id=1, replica_groups=mesh['gx'=16,'gy'=16,'gz'=2] {'gy','gz'}, dimensions={0} | all-to-all | bytes 131072 | tf_op jit(solution)/shard_map/all_to_all | solution.py:237
  97.8 0.8 scaled.1
  (1 shorter events, 0.0 us)
Async XLA Ops:
  0.0 1.7 %copy-start.1 = (bf16[1024,128]{1,0:T(8,128)(2,1)S(1)}, bf16[1024,128]{1,0:T(8,128)(2,1)}, u32[]{:S(2)}) copy-start(bf16[1024,128]{1,0:T(8,128)(2,1)} %u_ref.5) | copy-start | bytes 786436
  0.0 11.3 %copy-start = (bf16[64,64,512]{2,1,0:T(8,128)(2,1)S(1)}, bf16[64,64,512]{2,1,0:T(8,128)(2,1)}, u32[]{:S(2)}) copy-start(bf16[64,64,512]{2,1,0:T(8,128)(2,1)} %m_ref.3) | copy-start | bytes 12582916
  2.5 10.3 %collective-permute-start = (bf16[16,128,128]{2,1,0:T(8,128)(2,1)S(1)}, bf16[16,128,128]{2,1,0:T(8,128)(2,1)S(1)}, u32[]{:S(2)}, u32[]{:S(2)}) collective-permute-start(bf16[16,128,128]{2,1,0:T(8,128)(2,1)S(1)} %get-tuple-element.8), channel_id=1, source_target_pairs={{0,1},{1,0},{2,3},{3,2},{4,5},{5,4},{6,7},{7,6},{8,9},{9,8},{10,11... | collective-permute-start | bytes 1572872 | tf_op jit(solution)/shard_map/ppermute | solution.py:202

commit v4 on v3

--- a/solution.py
+++ b/solution.py
@@ -146,35 +146,48 @@
 
 
 def sum_kernel(in_ref, out_ref, mid_ref, low_ref, tail_ref):
-    total = jnp.sum(in_ref[...], axis=0)
+    total = jnp.sum(in_ref[...], axis=0) * (1.0 / 128.0)
     high = total.astype(BF16).astype(F32)
     rest = total - high
     mid = rest.astype(BF16).astype(F32)
     mid_ref[...] = mid
     low_ref[...] = rest - mid
-    tail_ref[...] = jnp.zeros(tail_ref.shape, F32)
+    for k in range(4):
+        group = high[8 * k : 8 * k + 8]
+        size = jnp.sum(group * group, axis=0, keepdims=True)
+        error = jnp.sum(group * rest[8 * k : 8 * k + 8], axis=0, keepdims=True)
+        ratio = jnp.where(size > 0.0, error / jnp.where(size > 0.0, size, 1.0), 0.0)
+        ratio = jnp.clip(ratio, -(2.0**-8), 2.0**-8)
+        for d in range(16):
+            tail_ref[d, k : k + 1, :] = ratio
     for d in range(16):
         for h in range(2):
-            tail_ref[d, h : h + 1, :] = mid_ref[16 * h + d : 16 * h + d + 1, :]
-            tail_ref[d, 2 + h : 3 + h, :] = low_ref[16 * h + d : 16 * h + d + 1, :]
+            tail_ref[d, 4 + h : 5 + h, :] = mid_ref[16 * h + d : 16 * h + d + 1, :]
+            tail_ref[d, 6 + h : 7 + h, :] = low_ref[16 * h + d : 16 * h + d + 1, :]
     high = jnp.broadcast_to(high[None], (16, 32, 128))
     out_ref[...] = jnp.concatenate([high, tail_ref[...]], axis=1).astype(BF16)
 
 
 def rows_kernel(idx_ref, in_ref, out_ref, v_ref):
-    v = jnp.sum(in_ref[...].astype(F32), axis=0)
+    parts = in_ref[...].astype(F32)
+    v = jnp.sum(parts, axis=0)
     v_ref[...] = v
-    squares = jnp.sum(v[0:32] * v[0:32], axis=0, keepdims=True)
+    squares = jnp.zeros((8, 128), F32)
+    for k in range(4):
+        group = parts[:, 8 * k : 8 * k + 8]
+        rows = v[8 * k : 8 * k + 8] + jnp.sum(group * parts[:, 32 + k : 33 + k], axis=0)
+        squares = squares + rows * rows
+    squares = jnp.sum(squares, axis=0, keepdims=True)
     block = idx_ref[0] // 2
     own = jnp.concatenate([v_ref[pl.ds(block, 1), :], v_ref[pl.ds(16 + block, 1), :]], axis=0)
-    own = own + (v[32:34] + v[34:36])
+    own = own + (v[36:38] + v[38:40])
     message = jnp.concatenate([own, squares, jnp.zeros((1, 128), F32)], axis=0)
     out_ref[...] = jnp.broadcast_to(message[None], out_ref.shape)
 
 
 def final_kernel(in_ref, out_ref):
-    total = jnp.sum(in_ref[pl.ds(2, 32, stride=4), :]) * (1.0 / (128.0 * 128.0))
-    scale = lax.rsqrt(total / (1024 * 128) + 1e-06) * (1.0 / 128.0)
+    total = jnp.sum(in_ref[pl.ds(2, 32, stride=4), :])
+    scale = lax.rsqrt(total / (1024 * 128) + 1e-06)
     for half in range(2):
         for core in range(2):
             for s in range(2):

time: 98.9 us -> 99 us (level)
  no operation moved by 1% of the time
where the time goes in v4:
time: 99 us; the launch traced here: 98.7 us
  blocking collectives  83.7 us (85%)
  starting transfers between devices  8.79 us (9%)
  Pallas kernels  5.63 us (6%)
    all_to_all x1, blocking collectives, local(): z = lax.all_to_all(z, 'gx', 0, 0, tiled=True)  25 us
    all_to_all x1, blocking collectives, local(): v = lax.all_to_all(v, plane, 0, 0, tiled=True)  15.4 us
    all_to_all x1, blocking collectives, local(): v = lax.all_to_all(v, 'gx', 0, 0, tiled=True)  14.7 us
    all_to_all x1, blocking collectives, local(): y = lax.all_to_all(y, 'gy', 0, 0, tiled=True)  12.9 us
    all_to_all x1, blocking collectives, local(): v = lax.all_to_all(v, 'gy', 0, 0, tiled=True)  10.6 us
    ppermute x1, starting transfers between devices, local(): came = lax.ppermute(there, 'gz', [(0, 1), (1, 0)])  8.79 us
    all_gather x1, blocking collectives, local(): z = lax.all_gather(z, 'gz', axis=0, tiled=True)  5.06 us
  transfers between devices with their start and end apart: 1, of which 1 were waited for; matrix products, arithmetic and copies ran while one was open for 0% of the time, Pallas kernels for 1%

profile of v4, /device:TPU:1, one launch (start us, length us, event | category | flops | bytes accessed | tf_op | source)
XLA Modules:
  0.0 98.7 jit_solution(13721207707558481609)
XLA Ops:
  0.0 0.0 copy-start.1
  0.0 0.0 copy-start
  0.0 1.7 %stage.1.theirs_ref = bf16[2,2,8,64,512]{4,3,2,1,0:T(8,128)(2,1)S(1)} custom-call(s32[1]{0:T(128)} %bitcast.idx_ref, bf16[64,64,512]{2,1,0:T(8,128)(2,1)} %m_ref.3), custom_call_target="tpu_custom_call" | custom-call | tf_op jit(solution)/shard_map/stage/pallas_call | solution.py:69
  1.7 0.0 copy-done.1
  1.7 0.8 y_there.1
  2.5 8.8 %collective-permute-start = (bf16[16,128,128]{2,1,0:T(8,128)(2,1)S(1)}, bf16[16,128,128]{2,1,0:T(8,128)(2,1)S(1)}, u32[]{:S(2)}, u32[]{:S(2)}) collective-permute-start(bf16[16,128,128]{2,1,0:T(8,128)(2,1)S(1)} %get-tuple-element.8), channel_id=1, source_target_pairs={{0,1},{1,0},{2,3},{3,2},{4,5},{5,4},{6,7},{7,6},{8,9},{9,8},{10,11... | collective-permute-start | bytes 1572872 | tf_op jit(solution)/shard_map/ppermute | solution.py:215
  11.3 0.0 copy-done
  11.3 1.1 %y_here.1 = bf16[16,128,128]{2,1,0:T(8,128)(2,1)S(1)} custom-call(s32[1]{0:T(128)} %bitcast.idx_ref, bf16[64,64,512]{2,1,0:T(8,128)(2,1)S(1)} %copy-done, bf16[128,512]{1,0:T(8,128)(2,1)S(1)} %get-tuple-element.7.ut_ref), custom_call_target="tpu_custom_call" | custom-call | tf_op jit(solution)/shard_map/y_here/pallas_call | solution.py:89
  12.5 0.4 collective-permute-done
  12.9 0.1 add_convert_fusion
  13.0 12.9 %all_to_all.25.y_ref = bf16[16,128,128]{2,1,0:T(8,128)(2,1)S(1)} all-to-all(bf16[16,128,128]{2,1,0:T(8,128)(2,1)S(1)} %add_convert_fusion), channel_id=1, replica_groups=mesh['gx'=16,'gy'=16,'gz'=2] {'gy'}, dimensions={0} | all-to-all | bytes 1048576 | tf_op jit(solution)/shard_map/all_to_all | solution.py:218
  25.9 0.5 z_block.1
  26.4 25.0 %all_to_all.26 = bf16[16,16,128]{2,1,0:T(8,128)(2,1)S(1)} all-to-all(bf16[16,16,128]{2,1,0:T(8,128)(2,1)S(1)} %z_block.1), channel_id=1, replica_groups=mesh['gx'=16,'gy'=16,'gz'=2] {'gx'}, dimensions={0} | all-to-all | bytes 131072 | tf_op jit(solution)/shard_map/all_to_all | solution.py:227
  51.5 5.1 %all_gather.3.z_ref = bf16[32,16,128]{2,1,0:T(8,128)(2,1)S(1)} all-gather(bf16[16,16,128]{2,1,0:T(8,128)(2,1)S(1)} %all_to_all.26), channel_id=1, replica_groups=mesh['gx'=16,'gy'=16,'gz'=2] {'gz'}, dimensions={0}, use_global_device_ids=true | all-gather | bytes 196608 | tf_op jit(solution)/shard_map/all_gather | solution.py:228
  56.5 0.5 v_part.1
  57.0 10.6 %all_to_all.27.in_ref = f32[16,32,128]{2,1,0:T(8,128)S(1)} all-to-all(f32[16,32,128]{2,1,0:T(8,128)S(1)} %v_part.1), channel_id=1, replica_groups=mesh['gx'=16,'gy'=16,'gz'=2] {'gy'}, dimensions={0} | all-to-all | bytes 524288 | tf_op jit(solution)/shard_map/all_to_all | solution.py:237
  67.6 0.1 v_sum_plane.1
  67.7 14.7 %all_to_all.28.in_ref = bf16[16,40,128]{2,1,0:T(8,128)(2,1)S(1)} all-to-all(bf16[16,40,128]{2,1,0:T(8,128)(2,1)S(1)} %v_sum_plane.1), channel_id=1, replica_groups=mesh['gx'=16,'gy'=16,'gz'=2] {'gx'}, dimensions={0} | all-to-all | bytes 327680 | tf_op jit(solution)/shard_map/all_to_all | solution.py:246
  82.4 0.1 v_rows.1
  82.5 15.4 %all_to_all.29 = f32[32,4,128]{2,1,0:T(4,128)S(1)} all-to-all(f32[32,4,128]{2,1,0:T(4,128)S(1)} %v_rows.1), channel_id=1, replica_groups=mesh['gx'=16,'gy'=16,'gz'=2] {'gy','gz'}, dimensions={0} | all-to-all | bytes 131072 | tf_op jit(solution)/shard_map/all_to_all | solution.py:250
  97.9 0.8 scaled.1
Async XLA Ops:
  0.0 1.7 %copy-start.1 = (bf16[1024,128]{1,0:T(8,128)(2,1)S(1)}, bf16[1024,128]{1,0:T(8,128)(2,1)}, u32[]{:S(2)}) copy-start(bf16[1024,128]{1,0:T(8,128)(2,1)} %u_ref.5) | copy-start | bytes 786436
  0.0 11.3 %copy-start = (bf16[64,64,512]{2,1,0:T(8,128)(2,1)S(1)}, bf16[64,64,512]{2,1,0:T(8,128)(2,1)}, u32[]{:S(2)}) copy-start(bf16[64,64,512]{2,1,0:T(8,128)(2,1)} %m_ref.3) | copy-start | bytes 12582916
  2.5 10.3 %collective-permute-start = (bf16[16,128,128]{2,1,0:T(8,128)(2,1)S(1)}, bf16[16,128,128]{2,1,0:T(8,128)(2,1)S(1)}, u32[]{:S(2)}, u32[]{:S(2)}) collective-permute-start(bf16[16,128,128]{2,1,0:T(8,128)(2,1)S(1)} %get-tuple-element.8), channel_id=1, source_target_pairs={{0,1},{1,0},{2,3},{3,2},{4,5},{5,4},{6,7},{7,6},{8,9},{9,8},{10,11... | collective-permute-start | bytes 1572872 | tf_op jit(solution)/shard_map/ppermute | solution.py:215

commit v5 on v4

--- a/solution.py
+++ b/solution.py
@@ -97,52 +97,33 @@
     )(idx, moment, ut)
 
 
-def z_kernel(y_ref, u_ref, out_ref, w_ref, z_ref):
-    w_ref[...] = jnp.zeros(w_ref.shape, BF16)
-    for s in range(16):
-        block = u_ref[64 * s : 64 * s + 64, :]
-        w_ref[128 * s : 128 * s + 64, 0:128] = block
-        w_ref[128 * s + 64 : 128 * s + 128, 128:256] = block
-    lhs = jnp.concatenate([y_ref[s] for s in range(16)], axis=1)
-    z = jnp.dot(lhs, w_ref[...], preferred_element_type=F32) * (1.0 / 32.0)
-    z_ref[0] = z[:, 0:128]
-    z_ref[1] = z[:, 128:256]
+def z_kernel(y_ref, u_ref, out_ref, z_ref):
+    lhs = []
+    for i2 in range(2):
+        cut = [y_ref[s][:, 64 * i2 : 64 * i2 + 64] for s in range(16)]
+        lhs.append(jnp.concatenate(cut, axis=1))
+    z = jnp.dot(jnp.concatenate(lhs, axis=0), u_ref[...], preferred_element_type=F32) * (1.0 / 32.0)
+    z_ref[0] = z[0:128]
+    z_ref[1] = z[128:256]
     for b in range(8):
-        zb = [z_ref[i2, pl.ds(b, 16, stride=8), :] for i2 in range(2)]
-        parts = []
-        for q in range(4):
-            cut = [
-                zb[i2][8 * iph : 8 * iph + 8, 32 * q : 32 * q + 32]
-                for i2 in range(2)
-                for iph in range(2)
-            ]
-            parts.append(jnp.concatenate(cut, axis=1))
-        for q2 in range(2):
-            block = jnp.concatenate(parts[2 * q2 : 2 * q2 + 2], axis=0).astype(BF16)
-            out_ref[2 * b + q2] = block
+        low, high = [z_ref[i2, pl.ds(b, 16, stride=8), :] for i2 in range(2)]
+        out_ref[2 * b] = jnp.concatenate([low[:, 0:64], high[:, 0:64]], axis=1).astype(BF16)
+        out_ref[2 * b + 1] = jnp.concatenate([low[:, 64:128], high[:, 64:128]], axis=1).astype(BF16)
 
 
 def v_kernel(idx_ref, z_ref, u_ref, out_ref, w_ref, v_ref):
     core = lax.rem(idx_ref[0], 2)
-    z = z_ref[...].astype(F32)
-    zt = jnp.concatenate([z[:, 8 * q : 8 * q + 8].reshape(256, 128) for q in range(2)], axis=1).astype(BF16)
-    u = u_ref[...].astype(F32).reshape(16, 2, 4, 8, 128)
-    uw = [jnp.concatenate([u[:, h, s].reshape(128, 128) for h in range(2)], axis=0) for s in range(4)]
-    uw = jnp.concatenate(uw, axis=1).astype(BF16)
+    u = u_ref[...].reshape(16, 4, 16, 128)
+    uw = [jnp.concatenate([u[:, 2 * h + i2].reshape(256, 128) for h in range(2)], axis=0) for i2 in range(2)]
+    uw = jnp.concatenate(uw, axis=1)
+    zt = z_ref[...]
     full = lax.dot_general(zt, uw, (((0,), (0,)), ((), ())), preferred_element_type=F32)
+    c = (full[0:64, 0:128] + full[64:128, 128:256]) * (1.0 / 32.0)
     w_ref[...] = jnp.zeros(w_ref.shape, BF16)
-    for q in range(2):
-        c = full[128 * q : 128 * q + 32, 0:128]
-        for s in range(1, 4):
-            c = c + full[128 * q + 32 * s : 128 * q + 32 * s + 32, 128 * s : 128 * s + 128]
-        c = (c * (1.0 / 32.0)).astype(BF16)
-        for s in range(2):
-            w_ref[pl.ds(pl.multiple_of(128 * q + 64 * core + 32 * s, 32), 32), 128 * s : 128 * s + 128] = c
-    v = jnp.dot(zt, w_ref[...], preferred_element_type=F32)
-    for s in range(2):
-        v_ref[s] = v[:, 128 * s : 128 * s + 128]
-        for row in range(8):
-            out_ref[8 * s + row] = v_ref[s, pl.ds(row, 32, stride=8), :]
+    w_ref[pl.ds(pl.multiple_of(64 * core, 64), 64), :] = c.astype(BF16)
+    v_ref[...] = jnp.dot(zt, w_ref[...], preferred_element_type=F32)
+    for ip in range(16):
+        out_ref[ip] = v_ref[pl.ds(ip, 32, stride=16), :]
 
 
 def sum_kernel(in_ref, out_ref, mid_ref, low_ref, tail_ref):
@@ -190,10 +171,8 @@
     scale = lax.rsqrt(total / (1024 * 128) + 1e-06)
     for half in range(2):
         for core in range(2):
-            for s in range(2):
-                rows = in_ref[pl.ds(64 * s + 4 * core + half, 8, stride=8), :]
-                first = 32 * half + 16 * core + 8 * s
-                out_ref[first : first + 8, :] = rows * scale
+            first = 32 * half + 16 * core
+            out_ref[first : first + 16, :] = in_ref[pl.ds(4 * core + half, 16, stride=8), :] * scale
 
 
 def call(kernel, out, specs, scratch, mib, name):
@@ -220,7 +199,7 @@
         z_kernel,
         ((16, 16, 128), BF16),
         [VMEM, VMEM],
-        [pltpu.VMEM((2048, 256), BF16), pltpu.VMEM((2, 128, 128), F32)],
+        [pltpu.VMEM((2, 128, 128), F32)],
         8,
         "z_block",
     )(y, factor)
@@ -230,10 +209,10 @@
         v_kernel,
         ((16, 32, 128), F32),
         [SMEM, VMEM, VMEM],
-        [pltpu.VMEM((256, 256), BF16), pltpu.VMEM((2, 256, 128), F32)],
+        [pltpu.VMEM((128, 128), BF16), pltpu.VMEM((512, 128), F32)],
         8,
         "v_part",
-    )(idx, z, factor)
+    )(idx, z.reshape(512, 128), factor)
     v = lax.all_to_all(v, "gy", 0, 0, tiled=True)
     v = call(
         sum_kernel,

time: 99 us -> 98.8 us (level)
  no operation moved by 1% of the time
where the time goes in v5:
time: 98.8 us; the launch traced here: 98.5 us
  blocking collectives  83.7 us (85%)
  starting transfers between devices  8.79 us (9%)
  Pallas kernels  5.51 us (6%)
    all_to_all x1, blocking collectives, local(): z = lax.all_to_all(z, 'gx', 0, 0, tiled=True)  25 us
    all_to_all x1, blocking collectives, local(): v = lax.all_to_all(v, plane, 0, 0, tiled=True)  15.4 us
    all_to_all x1, blocking collectives, local(): v = lax.all_to_all(v, 'gx', 0, 0, tiled=True)  14.7 us
    all_to_all x1, blocking collectives, local(): y = lax.all_to_all(y, 'gy', 0, 0, tiled=True)  12.9 us
    all_to_all x1, blocking collectives, local(): v = lax.all_to_all(v, 'gy', 0, 0, tiled=True)  10.6 us
    ppermute x1, starting transfers between devices, local(): came = lax.ppermute(there, 'gz', [(0, 1), (1, 0)])  8.79 us
    all_gather x1, blocking collectives, local(): z = lax.all_gather(z, 'gz', axis=0, tiled=True)  5.06 us
  transfers between devices with their start and end apart: 1, of which 1 were waited for; matrix products, arithmetic and copies ran while one was open for 0% of the time, Pallas kernels for 1%

profile of v5, /device:TPU:1, one launch (start us, length us, event | category | flops | bytes accessed | tf_op | source)
XLA Modules:
  0.0 98.5 jit_solution(14891153772170352067)
XLA Ops:
  0.0 0.0 copy-start.1
  0.0 0.0 copy-start
  0.0 1.7 %stage.1.theirs_ref = bf16[2,2,8,64,512]{4,3,2,1,0:T(8,128)(2,1)S(1)} custom-call(s32[1]{0:T(128)} %bitcast.idx_ref, bf16[64,64,512]{2,1,0:T(8,128)(2,1)} %m_ref.3), custom_call_target="tpu_custom_call" | custom-call | tf_op jit(solution)/shard_map/stage/pallas_call | solution.py:69
  1.7 0.0 copy-done.1
  1.7 0.8 y_there.1
  2.5 8.8 %collective-permute-start = (bf16[16,128,128]{2,1,0:T(8,128)(2,1)S(1)}, bf16[16,128,128]{2,1,0:T(8,128)(2,1)S(1)}, u32[]{:S(2)}, u32[]{:S(2)}) collective-permute-start(bf16[16,128,128]{2,1,0:T(8,128)(2,1)S(1)} %get-tuple-element.8), channel_id=1, source_target_pairs={{0,1},{1,0},{2,3},{3,2},{4,5},{5,4},{6,7},{7,6},{8,9},{9,8},{10,11... | collective-permute-start | bytes 1572872 | tf_op jit(solution)/shard_map/ppermute | solution.py:194
  11.3 0.0 copy-done
  11.3 1.1 %y_here.1 = bf16[16,128,128]{2,1,0:T(8,128)(2,1)S(1)} custom-call(s32[1]{0:T(128)} %bitcast.idx_ref, bf16[64,64,512]{2,1,0:T(8,128)(2,1)S(1)} %copy-done, bf16[128,512]{1,0:T(8,128)(2,1)S(1)} %get-tuple-element.7.ut_ref), custom_call_target="tpu_custom_call" | custom-call | tf_op jit(solution)/shard_map/y_here/pallas_call | solution.py:89
  12.5 0.4 collective-permute-done
  12.9 0.1 add_convert_fusion
  13.0 12.9 %all_to_all.25.y_ref = bf16[16,128,128]{2,1,0:T(8,128)(2,1)S(1)} all-to-all(bf16[16,128,128]{2,1,0:T(8,128)(2,1)S(1)} %add_convert_fusion), channel_id=1, replica_groups=mesh['gx'=16,'gy'=16,'gz'=2] {'gy'}, dimensions={0} | all-to-all | bytes 1048576 | tf_op jit(solution)/shard_map/all_to_all | solution.py:197
  25.9 0.4 z_block.1
  26.3 25.0 %all_to_all.26 = bf16[16,16,128]{2,1,0:T(8,128)(2,1)S(1)} all-to-all(bf16[16,16,128]{2,1,0:T(8,128)(2,1)S(1)} %z_block.1), channel_id=1, replica_groups=mesh['gx'=16,'gy'=16,'gz'=2] {'gx'}, dimensions={0} | all-to-all | bytes 131072 | tf_op jit(solution)/shard_map/all_to_all | solution.py:206
  51.4 5.1 %all_gather.3 = bf16[32,16,128]{2,1,0:T(8,128)(2,1)S(1)} all-gather(bf16[16,16,128]{2,1,0:T(8,128)(2,1)S(1)} %all_to_all.26), channel_id=1, replica_groups=mesh['gx'=16,'gy'=16,'gz'=2] {'gz'}, dimensions={0}, use_global_device_ids=true | all-gather | bytes 196608 | tf_op jit(solution)/shard_map/all_gather | solution.py:207
  56.4 0.5 v_part.1
  56.9 10.6 %all_to_all.27.in_ref = f32[16,32,128]{2,1,0:T(8,128)S(1)} all-to-all(f32[16,32,128]{2,1,0:T(8,128)S(1)} %v_part.1), channel_id=1, replica_groups=mesh['gx'=16,'gy'=16,'gz'=2] {'gy'}, dimensions={0} | all-to-all | bytes 524288 | tf_op jit(solution)/shard_map/all_to_all | solution.py:216
  67.5 0.1 v_sum_plane.1
  67.6 14.7 %all_to_all.28.in_ref = bf16[16,40,128]{2,1,0:T(8,128)(2,1)S(1)} all-to-all(bf16[16,40,128]{2,1,0:T(8,128)(2,1)S(1)} %v_sum_plane.1), channel_id=1, replica_groups=mesh['gx'=16,'gy'=16,'gz'=2] {'gx'}, dimensions={0} | all-to-all | bytes 327680 | tf_op jit(solution)/shard_map/all_to_all | solution.py:225
  82.3 0.1 v_rows.1
  82.4 15.4 %all_to_all.29 = f32[32,4,128]{2,1,0:T(4,128)S(1)} all-to-all(f32[32,4,128]{2,1,0:T(4,128)S(1)} %v_rows.1), channel_id=1, replica_groups=mesh['gx'=16,'gy'=16,'gz'=2] {'gy','gz'}, dimensions={0} | all-to-all | bytes 131072 | tf_op jit(solution)/shard_map/all_to_all | solution.py:229
  97.8 0.8 scaled.1
Async XLA Ops:
  0.0 1.7 %copy-start.1 = (bf16[1024,128]{1,0:T(8,128)(2,1)S(1)}, bf16[1024,128]{1,0:T(8,128)(2,1)}, u32[]{:S(2)}) copy-start(bf16[1024,128]{1,0:T(8,128)(2,1)} %u_ref.5) | copy-start | bytes 786436
  0.0 11.3 %copy-start = (bf16[64,64,512]{2,1,0:T(8,128)(2,1)S(1)}, bf16[64,64,512]{2,1,0:T(8,128)(2,1)}, u32[]{:S(2)}) copy-start(bf16[64,64,512]{2,1,0:T(8,128)(2,1)} %m_ref.3) | copy-start | bytes 12582916
  2.5 10.3 %collective-permute-start = (bf16[16,128,128]{2,1,0:T(8,128)(2,1)S(1)}, bf16[16,128,128]{2,1,0:T(8,128)(2,1)S(1)}, u32[]{:S(2)}, u32[]{:S(2)}) collective-permute-start(bf16[16,128,128]{2,1,0:T(8,128)(2,1)S(1)} %get-tuple-element.8), channel_id=1, source_target_pairs={{0,1},{1,0},{2,3},{3,2},{4,5},{5,4},{6,7},{7,6},{8,9},{9,8},{10,11... | collective-permute-start | bytes 1572872 | tf_op jit(solution)/shard_map/ppermute | solution.py:194

commit v6 on v5

--- a/solution.py
+++ b/solution.py
@@ -1,3 +1,5 @@
+import functools
+
 import jax
 import jax.numpy as jnp
 from jax import lax
@@ -45,8 +47,8 @@
         y_store(ut, rows, CHUNK * t + p, out_ref)
 
 
-def stage_kernel(idx_ref, m_ref, theirs_ref, sem):
-    for copy in y_copies(1 - lax.rem(idx_ref[0], 2), m_ref, theirs_ref, sem):
+def stage_kernel(first_core_ref, m_ref, theirs_ref, sem):
+    for copy in y_copies(first_core_ref[0], m_ref, theirs_ref, sem):
         copy.wait()
 
 
@@ -65,7 +67,7 @@
         y_chunk(t, ut_ref[...], buf, out_ref)
 
 
-def y_there(idx, moment, factor):
+def y_there(idx, first_core, moment, factor):
     theirs = pl.pallas_call(
         stage_kernel,
         out_shape=jax.ShapeDtypeStruct(HALF, BF16),
@@ -74,7 +76,7 @@
         scratch_shapes=[pltpu.SemaphoreType.DMA((CHUNKS, 2))],
         compiler_params=params(48),
         name="stage",
-    )(idx, moment)
+    )(first_core, moment)
     return pl.pallas_call(
         y_there_kernel,
         out_shape=[jax.ShapeDtypeStruct((16, 128, 128), BF16), jax.ShapeDtypeStruct((128, 512), BF16)],
@@ -111,68 +113,71 @@
         out_ref[2 * b + 1] = jnp.concatenate([low[:, 64:128], high[:, 64:128]], axis=1).astype(BF16)
 
 
-def v_kernel(idx_ref, z_ref, u_ref, out_ref, w_ref, v_ref):
-    core = lax.rem(idx_ref[0], 2)
+SHARES = (((0, 0),), ((0, 1), (1, 0), (1, 1)))
+
+
+def v_kernel(share, z_ref, u_ref, out_ref, w_ref, v_ref):
     u = u_ref[...].reshape(16, 4, 16, 128)
     uw = [jnp.concatenate([u[:, 2 * h + i2].reshape(256, 128) for h in range(2)], axis=0) for i2 in range(2)]
     uw = jnp.concatenate(uw, axis=1)
-    zt = z_ref[...]
-    full = lax.dot_general(zt, uw, (((0,), (0,)), ((), ())), preferred_element_type=F32)
-    c = (full[0:64, 0:128] + full[64:128, 128:256]) * (1.0 / 32.0)
+    full = lax.dot_general(z_ref[...], uw, (((0,), (0,)), ((), ())), preferred_element_type=F32)
+    c = ((full[0:64, 0:128] + full[64:128, 128:256]) * (1.0 / 32.0)).astype(BF16)
     w_ref[...] = jnp.zeros(w_ref.shape, BF16)
-    w_ref[pl.ds(pl.multiple_of(64 * core, 64), 64), :] = c.astype(BF16)
-    v_ref[...] = jnp.dot(zt, w_ref[...], preferred_element_type=F32)
-    for ip in range(16):
-        out_ref[ip] = v_ref[pl.ds(ip, 32, stride=16), :]
-
-
-def sum_kernel(in_ref, out_ref, mid_ref, low_ref, tail_ref):
+    w_ref[0, 0:64] = c
+    w_ref[1, 64:128] = c
+    for n, (half, i2) in enumerate(share):
+        rows = z_ref[256 * half : 256 * half + 256, :]
+        v_ref[n] = jnp.dot(rows, w_ref[i2], preferred_element_type=F32)
+        for ip in range(16):
+            out_ref[ip, 16 * n : 16 * n + 16, :] = v_ref[n, pl.ds(ip, 16, stride=16), :]
+
+
+def sum_kernel(in_ref, out_ref, mid_ref, tail_ref):
     total = jnp.sum(in_ref[...], axis=0) * (1.0 / 128.0)
+    count = total.shape[0] // 16
     high = total.astype(BF16).astype(F32)
     rest = total - high
-    mid = rest.astype(BF16).astype(F32)
-    mid_ref[...] = mid
-    low_ref[...] = rest - mid
-    for k in range(4):
-        group = high[8 * k : 8 * k + 8]
+    mid_ref[...] = rest
+    tail_ref[...] = jnp.zeros(tail_ref.shape, F32)
+    for n in range(count):
+        group = high[16 * n : 16 * n + 16]
         size = jnp.sum(group * group, axis=0, keepdims=True)
-        error = jnp.sum(group * rest[8 * k : 8 * k + 8], axis=0, keepdims=True)
+        error = jnp.sum(group * rest[16 * n : 16 * n + 16], axis=0, keepdims=True)
         ratio = jnp.where(size > 0.0, error / jnp.where(size > 0.0, size, 1.0), 0.0)
         ratio = jnp.clip(ratio, -(2.0**-8), 2.0**-8)
         for d in range(16):
-            tail_ref[d, k : k + 1, :] = ratio
-    for d in range(16):
-        for h in range(2):
-            tail_ref[d, 4 + h : 5 + h, :] = mid_ref[16 * h + d : 16 * h + d + 1, :]
-            tail_ref[d, 6 + h : 7 + h, :] = low_ref[16 * h + d : 16 * h + d + 1, :]
-    high = jnp.broadcast_to(high[None], (16, 32, 128))
+            tail_ref[d, n : n + 1, :] = ratio
+            tail_ref[d, count + n : count + n + 1, :] = mid_ref[16 * n + d : 16 * n + d + 1, :]
+    high = jnp.broadcast_to(high[None], (16,) + high.shape)
     out_ref[...] = jnp.concatenate([high, tail_ref[...]], axis=1).astype(BF16)
 
 
-def rows_kernel(idx_ref, in_ref, out_ref, v_ref):
+def rows_kernel(count, idx_ref, in_ref, out_ref, v_ref):
     parts = in_ref[...].astype(F32)
     v = jnp.sum(parts, axis=0)
     v_ref[...] = v
-    squares = jnp.zeros((8, 128), F32)
-    for k in range(4):
-        group = parts[:, 8 * k : 8 * k + 8]
-        rows = v[8 * k : 8 * k + 8] + jnp.sum(group * parts[:, 32 + k : 33 + k], axis=0)
+    first = 16 * count
+    squares = jnp.zeros((16, 128), F32)
+    for n in range(count):
+        group = parts[:, 16 * n : 16 * n + 16]
+        rows = v[16 * n : 16 * n + 16] + jnp.sum(group * parts[:, first + n : first + n + 1], axis=0)
         squares = squares + rows * rows
     squares = jnp.sum(squares, axis=0, keepdims=True)
     block = idx_ref[0] // 2
-    own = jnp.concatenate([v_ref[pl.ds(block, 1), :], v_ref[pl.ds(16 + block, 1), :]], axis=0)
-    own = own + (v[36:38] + v[38:40])
-    message = jnp.concatenate([own, squares, jnp.zeros((1, 128), F32)], axis=0)
+    own = jnp.concatenate([v_ref[pl.ds(16 * n + block, 1), :] for n in range(count)], axis=0)
+    own = own + v[first + count : first + 2 * count]
+    own = [own] if count == 3 else [own, jnp.zeros((3 - count, 128), F32)]
+    message = jnp.concatenate(own + [squares], axis=0)
     out_ref[...] = jnp.broadcast_to(message[None], out_ref.shape)
 
 
 def final_kernel(in_ref, out_ref):
-    total = jnp.sum(in_ref[pl.ds(2, 32, stride=4), :])
+    total = jnp.sum(in_ref[pl.ds(3, 32, stride=4), :])
     scale = lax.rsqrt(total / (1024 * 128) + 1e-06)
-    for half in range(2):
-        for core in range(2):
-            first = 32 * half + 16 * core
-            out_ref[first : first + 16, :] = in_ref[pl.ds(4 * core + half, 16, stride=8), :] * scale
+    for core, share in enumerate(SHARES):
+        for n, (half, i2) in enumerate(share):
+            first = 32 * half + 16 * i2
+            out_ref[first : first + 16, :] = in_ref[pl.ds(4 * core + n, 16, stride=8), :] * scale
 
 
 def call(kernel, out, specs, scratch, mib, name):
@@ -187,10 +192,42 @@
     )
 
 
+def v_share(share, idx, z, factor):
+    count = len(share)
+    tail = -(-2 * count // 8) * 8
+    v = call(
+        functools.partial(v_kernel, share),
+        ((16, 16 * count, 128), F32),
+        [VMEM, VMEM],
+        [pltpu.VMEM((2, 128, 128), BF16), pltpu.VMEM((count, 256, 128), F32)],
+        8,
+        "v_part",
+    )(z, factor)
+    v = lax.all_to_all(v, "gy", 0, 0, tiled=True)
+    v = call(
+        sum_kernel,
+        ((16, 16 * count + tail, 128), BF16),
+        [VMEM],
+        [pltpu.VMEM((16 * count, 128), F32), pltpu.VMEM((16, tail, 128), F32)],
+        8,
+        "v_sum_plane",
+    )(v)
+    v = lax.all_to_all(v, "gx", 0, 0, tiled=True)
+    return call(
+        functools.partial(rows_kernel, count),
+        ((32, 4, 128), F32),
+        [SMEM, VMEM],
+        [pltpu.VMEM((16 * count + tail, 128), F32)],
+        8,
+        "v_rows",
+    )(idx, v)
+
+
 def local(moment, factor):
     plane = ("gy", "gz")
     idx = (2 * lax.axis_index("gx") + lax.axis_index("gz")).astype(jnp.int32).reshape(1)
-    there, ut = y_there(idx, moment, factor)
+    first_core = lax.rem(idx[0], 2) == 0
+    there, ut = y_there(idx, first_core.astype(jnp.int32).reshape(1), moment, factor)
     came = lax.ppermute(there, "gz", [(0, 1), (1, 0)])
     here = y_here(idx, moment, ut)
     y = (here.astype(F32) + came.astype(F32)).astype(BF16)
@@ -205,27 +242,8 @@
     )(y, factor)
     z = lax.all_to_all(z, "gx", 0, 0, tiled=True)
     z = lax.all_gather(z, "gz", axis=0, tiled=True)
-    v = call(
-        v_kernel,
-        ((16, 32, 128), F32),
-        [SMEM, VMEM, VMEM],
-        [pltpu.VMEM((128, 128), BF16), pltpu.VMEM((512, 128), F32)],
-        8,
-        "v_part",
-    )(idx, z.reshape(512, 128), factor)
-    v = lax.all_to_all(v, "gy", 0, 0, tiled=True)
-    v = call(
-        sum_kernel,
-        ((16, 40, 128), BF16),
-        [VMEM],
-        [pltpu.VMEM((32, 128), F32), pltpu.VMEM((32, 128), F32), pltpu.VMEM((16, 8, 128), F32)],
-        8,
-        "v_sum_plane",
-    )(v)
-    v = lax.all_to_all(v, "gx", 0, 0, tiled=True)
-    v = call(
-        rows_kernel, ((32, 4, 128), F32), [SMEM, VMEM], [pltpu.VMEM((40, 128), F32)], 8, "v_rows"
-    )(idx, v)
+    branches = [functools.partial(v_share, share) for share in SHARES]
+    v = lax.cond(first_core, *branches, idx, z.reshape(512, 128), factor)
     v = lax.all_to_all(v, plane, 0, 0, tiled=True)
     return call(final_kernel, ((64, 128), F32), [VMEM], [], 8, "scaled")(v.reshape(128, 128))
 

time: 98.8 us -> 98.2 us (level)
    all_to_all x1, blocking collectives: 15.4 us -> 12 us  [local(): v = lax.all_to_all(v, plane, 0, 0, tiled=True)]
    all_to_all x2, blocking collectives: 25.3 us -> 27.8 us  [the longest x1 16 us: v_share(): v = lax.all_to_all(v, 'gx', 0, 0, tiled=True)]
where the time goes in v6:
time: 98.2 us; the launch traced here: 97.7 us
  blocking collectives  82.8 us (84%)
  starting transfers between devices  8.79 us (9%)
  Pallas kernels  5.58 us (6%)
    all_to_all x1, blocking collectives, local(): z = lax.all_to_all(z, 'gx', 0, 0, tiled=True)  25 us
    all_to_all x1, blocking collectives, v_share(): v = lax.all_to_all(v, 'gx', 0, 0, tiled=True)  16 us
    all_to_all x1, blocking collectives, local(): y = lax.all_to_all(y, 'gy', 0, 0, tiled=True)  12.9 us
    all_to_all x1, blocking collectives, local(): v = lax.all_to_all(v, plane, 0, 0, tiled=True)  12 us
    all_to_all x1, blocking collectives, v_share(): v = lax.all_to_all(v, 'gy', 0, 0, tiled=True)  11.8 us
    ppermute x1, starting transfers between devices, local(): came = lax.ppermute(there, 'gz', [(0, 1), (1, 0)])  8.79 us
    all_gather x1, blocking collectives, local(): z = lax.all_gather(z, 'gz', axis=0, tiled=True)  5.06 us
  transfers between devices with their start and end apart: 1, of which 1 were waited for; matrix products, arithmetic and copies ran while one was open for 0% of the time, Pallas kernels for 1%

profile of v6, /device:TPU:1, one launch (start us, length us, event | category | flops | bytes accessed | tf_op | source)
XLA Modules:
  0.0 97.7 jit_solution(12543084273561956463)
XLA Ops:
  0.0 0.0 copy-start.1
  0.0 0.0 copy-start
  0.0 1.7 %stage.1.theirs_ref = bf16[2,2,8,64,512]{4,3,2,1,0:T(8,128)(2,1)S(1)} custom-call(s32[1]{0:T(128)} %bitcast.1.first_core_ref, bf16[64,64,512]{2,1,0:T(8,128)(2,1)} %m_ref.3), custom_call_target="tpu_custom_call" | custom-call | tf_op jit(solution)/shard_map/stage/pallas_call | solution.py:71
  1.7 0.0 copy-done.1
  1.7 0.8 y_there.1
  2.5 8.8 %collective-permute-start = (bf16[16,128,128]{2,1,0:T(8,128)(2,1)S(1)}, bf16[16,128,128]{2,1,0:T(8,128)(2,1)S(1)}, u32[]{:S(2)}, u32[]{:S(2)}) collective-permute-start(bf16[16,128,128]{2,1,0:T(8,128)(2,1)S(1)} %get-tuple-element.29), channel_id=1, source_target_pairs={{0,1},{1,0},{2,3},{3,2},{4,5},{5,4},{6,7},{7,6},{8,9},{9,8},{10,11... | collective-permute-start | bytes 1572872 | tf_op jit(solution)/shard_map/ppermute | solution.py:231
  11.3 0.0 copy-done
  11.4 1.1 %y_here.1 = bf16[16,128,128]{2,1,0:T(8,128)(2,1)S(1)} custom-call(s32[1]{0:T(128)} %bitcast.idx_ref, bf16[64,64,512]{2,1,0:T(8,128)(2,1)S(1)} %copy-done, bf16[128,512]{1,0:T(8,128)(2,1)S(1)} %get-tuple-element.28.ut_ref), custom_call_target="tpu_custom_call" | custom-call | tf_op jit(solution)/shard_map/y_here/pallas_call | solution.py:91
  12.5 0.4 collective-permute-done
  12.9 0.1 add_convert_fusion
  13.0 12.9 %all_to_all.35.y_ref = bf16[16,128,128]{2,1,0:T(8,128)(2,1)S(1)} all-to-all(bf16[16,128,128]{2,1,0:T(8,128)(2,1)S(1)} %add_convert_fusion), channel_id=1, replica_groups=mesh['gx'=16,'gy'=16,'gz'=2] {'gy'}, dimensions={0} | all-to-all | bytes 1048576 | tf_op jit(solution)/shard_map/all_to_all | solution.py:234
  25.9 0.4 z_block.1
  26.3 25.0 %all_to_all.36 = bf16[16,16,128]{2,1,0:T(8,128)(2,1)S(1)} all-to-all(bf16[16,16,128]{2,1,0:T(8,128)(2,1)S(1)} %z_block.1), channel_id=1, replica_groups=mesh['gx'=16,'gy'=16,'gz'=2] {'gx'}, dimensions={0} | all-to-all | bytes 131072 | tf_op jit(solution)/shard_map/all_to_all | solution.py:243
  51.4 5.1 %all_gather.3 = bf16[32,16,128]{2,1,0:T(8,128)(2,1)S(1)} all-gather(bf16[16,16,128]{2,1,0:T(8,128)(2,1)S(1)} %all_to_all.36), channel_id=1, replica_groups=mesh['gx'=16,'gy'=16,'gz'=2] {'gz'}, dimensions={0}, use_global_device_ids=true | all-gather | bytes 196608 | tf_op jit(solution)/shard_map/all_gather | solution.py:244
  56.4 28.5 %conditional.1 = (f32[32,4,128]{2,1,0:T(4,128)S(1)}) conditional(s32[]{:T(128)} %convert_element_type.13, (bf16[512,128]{1,0:T(8,128)(2,1)S(1)}, bf16[1024,128]{1,0:T(8,128)(2,1)S(1)}, s32[1]{0:T(128)}) %tuple.16, (bf16[512,128]{1,0:T(8,128)(2,1)S(1)}, bf16[1024,128]{1,0:T(8,128)(2,1)S(1)}, s32[1]{0:T(128)}) %tuple.17), branch_computations={%region_0.0_spmd, %region_1.0_spmd} | conditional | bytes 1245192 | solution.py:246
  56.4 0.5 v_part.2
  57.0 11.8 %all_to_all.31.in_ref = f32[16,48,128]{2,1,0:T(8,128)S(1)} all-to-all(f32[16,48,128]{2,1,0:T(8,128)S(1)} %v_part.2), channel_id=1, replica_groups=mesh['gx'=16,'gy'=16,'gz'=2] {'gy'}, dimensions={0} | all-to-all | bytes 786432 | tf_op jit(solution)/shard_map/cond/branch_0_fun/all_to_all | solution.py:206
  68.7 0.1 v_sum_plane.2
  68.8 16.0 %all_to_all.32.in_ref = bf16[16,56,128]{2,1,0:T(8,128)(2,1)S(1)} all-to-all(bf16[16,56,128]{2,1,0:T(8,128)(2,1)S(1)} %v_sum_plane.2), channel_id=1, replica_groups=mesh['gx'=16,'gy'=16,'gz'=2] {'gx'}, dimensions={0} | all-to-all | bytes 458752 | tf_op jit(solution)/shard_map/cond/branch_0_fun/all_to_all | solution.py:215
  84.8 0.1 v_rows.2
  84.9 12.0 %all_to_all.37 = f32[32,4,128]{2,1,0:T(4,128)S(1)} all-to-all(f32[32,4,128]{2,1,0:T(4,128)S(1)} %get-tuple-element.30), channel_id=1, replica_groups=mesh['gx'=16,'gy'=16,'gz'=2] {'gy','gz'}, dimensions={0} | all-to-all | bytes 131072 | tf_op jit(solution)/shard_map/all_to_all | solution.py:247
  96.9 0.8 scaled.1
Async XLA Ops:
  0.0 1.7 %copy-start.1 = (bf16[1024,128]{1,0:T(8,128)(2,1)S(1)}, bf16[1024,128]{1,0:T(8,128)(2,1)}, u32[]{:S(2)}) copy-start(bf16[1024,128]{1,0:T(8,128)(2,1)} %u_ref.3) | copy-start | bytes 786436
  0.0 11.3 %copy-start = (bf16[64,64,512]{2,1,0:T(8,128)(2,1)S(1)}, bf16[64,64,512]{2,1,0:T(8,128)(2,1)}, u32[]{:S(2)}) copy-start(bf16[64,64,512]{2,1,0:T(8,128)(2,1)} %m_ref.3) | copy-start | bytes 12582916
  2.5 10.3 %collective-permute-start = (bf16[16,128,128]{2,1,0:T(8,128)(2,1)S(1)}, bf16[16,128,128]{2,1,0:T(8,128)(2,1)S(1)}, u32[]{:S(2)}, u32[]{:S(2)}) collective-permute-start(bf16[16,128,128]{2,1,0:T(8,128)(2,1)S(1)} %get-tuple-element.29), channel_id=1, source_target_pairs={{0,1},{1,0},{2,3},{3,2},{4,5},{5,4},{6,7},{7,6},{8,9},{9,8},{10,11... | collective-permute-start | bytes 1572872 | tf_op jit(solution)/shard_map/ppermute | solution.py:231

commit v7 on v6

--- a/solution.py
+++ b/solution.py
@@ -172,7 +172,8 @@
 
 
 def final_kernel(in_ref, out_ref):
-    total = jnp.sum(in_ref[pl.ds(3, 32, stride=4), :])
+    total = jnp.sum(in_ref[pl.ds(3, 32, stride=4), :], axis=0, keepdims=True)
+    total = jnp.sum(total, axis=1, keepdims=True)
     scale = lax.rsqrt(total / (1024 * 128) + 1e-06)
     for core, share in enumerate(SHARES):
         for n, (half, i2) in enumerate(share):

time: 98.2 us -> 98.1 us (level)
  no operation moved by 1% of the time
where the time goes in v7:
time: 98.1 us; the launch traced here: 97.7 us
  blocking collectives  82.8 us (84%)
  starting transfers between devices  8.79 us (9%)
  Pallas kernels  5.51 us (6%)
    all_to_all x1, blocking collectives, local(): z = lax.all_to_all(z, 'gx', 0, 0, tiled=True)  25 us
    all_to_all x1, blocking collectives, v_share(): v = lax.all_to_all(v, 'gx', 0, 0, tiled=True)  16 us
    all_to_all x1, blocking collectives, local(): y = lax.all_to_all(y, 'gy', 0, 0, tiled=True)  12.9 us
    all_to_all x1, blocking collectives, local(): v = lax.all_to_all(v, plane, 0, 0, tiled=True)  12 us
    all_to_all x1, blocking collectives, v_share(): v = lax.all_to_all(v, 'gy', 0, 0, tiled=True)  11.8 us
    ppermute x1, starting transfers between devices, local(): came = lax.ppermute(there, 'gz', [(0, 1), (1, 0)])  8.79 us
    all_gather x1, blocking collectives, local(): z = lax.all_gather(z, 'gz', axis=0, tiled=True)  5.06 us
  transfers between devices with their start and end apart: 1, of which 1 were waited for; matrix products, arithmetic and copies ran while one was open for 0% of the time, Pallas kernels for 1%

profile of v7, /device:TPU:1, one launch (start us, length us, event | category | flops | bytes accessed | tf_op | source)
XLA Modules:
  0.0 97.7 jit_solution(6705120120921940935)
XLA Ops:
  0.0 0.0 copy-start.1
  0.0 0.0 copy-start
  0.0 1.7 %stage.1.theirs_ref = bf16[2,2,8,64,512]{4,3,2,1,0:T(8,128)(2,1)S(1)} custom-call(s32[1]{0:T(128)} %bitcast.1.first_core_ref, bf16[64,64,512]{2,1,0:T(8,128)(2,1)} %m_ref.3), custom_call_target="tpu_custom_call" | custom-call | tf_op jit(solution)/shard_map/stage/pallas_call | solution.py:71
  1.7 0.0 copy-done.1
  1.7 0.8 y_there.1
  2.5 8.8 %collective-permute-start = (bf16[16,128,128]{2,1,0:T(8,128)(2,1)S(1)}, bf16[16,128,128]{2,1,0:T(8,128)(2,1)S(1)}, u32[]{:S(2)}, u32[]{:S(2)}) collective-permute-start(bf16[16,128,128]{2,1,0:T(8,128)(2,1)S(1)} %get-tuple-element.29), channel_id=1, source_target_pairs={{0,1},{1,0},{2,3},{3,2},{4,5},{5,4},{6,7},{7,6},{8,9},{9,8},{10,11... | collective-permute-start | bytes 1572872 | tf_op jit(solution)/shard_map/ppermute | solution.py:232
  11.3 0.0 copy-done
  11.4 1.1 %y_here.1 = bf16[16,128,128]{2,1,0:T(8,128)(2,1)S(1)} custom-call(s32[1]{0:T(128)} %bitcast.idx_ref, bf16[64,64,512]{2,1,0:T(8,128)(2,1)S(1)} %copy-done, bf16[128,512]{1,0:T(8,128)(2,1)S(1)} %get-tuple-element.28.ut_ref), custom_call_target="tpu_custom_call" | custom-call | tf_op jit(solution)/shard_map/y_here/pallas_call | solution.py:91
  12.5 0.4 collective-permute-done
  12.9 0.1 add_convert_fusion
  13.0 12.9 %all_to_all.35.y_ref = bf16[16,128,128]{2,1,0:T(8,128)(2,1)S(1)} all-to-all(bf16[16,128,128]{2,1,0:T(8,128)(2,1)S(1)} %add_convert_fusion), channel_id=1, replica_groups=mesh['gx'=16,'gy'=16,'gz'=2] {'gy'}, dimensions={0} | all-to-all | bytes 1048576 | tf_op jit(solution)/shard_map/all_to_all | solution.py:235
  25.9 0.4 z_block.1
  26.3 25.0 %all_to_all.36 = bf16[16,16,128]{2,1,0:T(8,128)(2,1)S(1)} all-to-all(bf16[16,16,128]{2,1,0:T(8,128)(2,1)S(1)} %z_block.1), channel_id=1, replica_groups=mesh['gx'=16,'gy'=16,'gz'=2] {'gx'}, dimensions={0} | all-to-all | bytes 131072 | tf_op jit(solution)/shard_map/all_to_all | solution.py:244
  51.4 5.1 %all_gather.3 = bf16[32,16,128]{2,1,0:T(8,128)(2,1)S(1)} all-gather(bf16[16,16,128]{2,1,0:T(8,128)(2,1)S(1)} %all_to_all.36), channel_id=1, replica_groups=mesh['gx'=16,'gy'=16,'gz'=2] {'gz'}, dimensions={0}, use_global_device_ids=true | all-gather | bytes 196608 | tf_op jit(solution)/shard_map/all_gather | solution.py:245
  56.4 28.5 %conditional.1 = (f32[32,4,128]{2,1,0:T(4,128)S(1)}) conditional(s32[]{:T(128)} %convert_element_type.13, (bf16[512,128]{1,0:T(8,128)(2,1)S(1)}, bf16[1024,128]{1,0:T(8,128)(2,1)S(1)}, s32[1]{0:T(128)}) %tuple.16, (bf16[512,128]{1,0:T(8,128)(2,1)S(1)}, bf16[1024,128]{1,0:T(8,128)(2,1)S(1)}, s32[1]{0:T(128)}) %tuple.17), branch_computations={%region_0.0_spmd, %region_1.0_spmd} | conditional | bytes 1245192 | solution.py:247
  56.4 0.5 v_part.2
  57.0 11.8 %all_to_all.31.in_ref = f32[16,48,128]{2,1,0:T(8,128)S(1)} all-to-all(f32[16,48,128]{2,1,0:T(8,128)S(1)} %v_part.2), channel_id=1, replica_groups=mesh['gx'=16,'gy'=16,'gz'=2] {'gy'}, dimensions={0} | all-to-all | bytes 786432 | tf_op jit(solution)/shard_map/cond/branch_0_fun/all_to_all | solution.py:207
  68.7 0.1 v_sum_plane.2
  68.8 16.0 %all_to_all.32.in_ref = bf16[16,56,128]{2,1,0:T(8,128)(2,1)S(1)} all-to-all(bf16[16,56,128]{2,1,0:T(8,128)(2,1)S(1)} %v_sum_plane.2), channel_id=1, replica_groups=mesh['gx'=16,'gy'=16,'gz'=2] {'gx'}, dimensions={0} | all-to-all | bytes 458752 | tf_op jit(solution)/shard_map/cond/branch_0_fun/all_to_all | solution.py:216
  84.8 0.1 v_rows.2
  84.9 12.0 %all_to_all.37 = f32[32,4,128]{2,1,0:T(4,128)S(1)} all-to-all(f32[32,4,128]{2,1,0:T(4,128)S(1)} %get-tuple-element.30), channel_id=1, replica_groups=mesh['gx'=16,'gy'=16,'gz'=2] {'gy','gz'}, dimensions={0} | all-to-all | bytes 131072 | tf_op jit(solution)/shard_map/all_to_all | solution.py:248
  96.9 0.7 scaled.1
Async XLA Ops:
  0.0 1.7 %copy-start.1 = (bf16[1024,128]{1,0:T(8,128)(2,1)S(1)}, bf16[1024,128]{1,0:T(8,128)(2,1)}, u32[]{:S(2)}) copy-start(bf16[1024,128]{1,0:T(8,128)(2,1)} %u_ref.3) | copy-start | bytes 786436
  0.0 11.3 %copy-start = (bf16[64,64,512]{2,1,0:T(8,128)(2,1)S(1)}, bf16[64,64,512]{2,1,0:T(8,128)(2,1)}, u32[]{:S(2)}) copy-start(bf16[64,64,512]{2,1,0:T(8,128)(2,1)} %m_ref.3) | copy-start | bytes 12582916
  2.5 10.3 %collective-permute-start = (bf16[16,128,128]{2,1,0:T(8,128)(2,1)S(1)}, bf16[16,128,128]{2,1,0:T(8,128)(2,1)S(1)}, u32[]{:S(2)}, u32[]{:S(2)}) collective-permute-start(bf16[16,128,128]{2,1,0:T(8,128)(2,1)S(1)} %get-tuple-element.29), channel_id=1, source_target_pairs={{0,1},{1,0},{2,3},{3,2},{4,5},{5,4},{6,7},{7,6},{8,9},{9,8},{10,11... | collective-permute-start | bytes 1572872 | tf_op jit(solution)/shard_map/ppermute | solution.py:232
